TPU v7x, 256 devices: a whole 4x4x8 slice. The times are simulated.
256 devices in a mesh: seq: 16 (over z, y_lo), tensor: 16 (over x, y_hi, core).
Axes of the slice: x: 4, y: 4 (y_hi: 2, y_lo: 2; y = y_hi * 2 + y_lo), z: 8, core: 2. Of those that a mesh axis runs over, the one named last changes fastest.
Arguments:
- tokens: bfloat16 [2048, 8192], P('tensor', 'seq'), may hold values from -6 to 6
- gate_codes: bfloat16 [8192, 28672], P('seq', 'tensor'), may hold values from -127 to 127, as said below
- up_codes: bfloat16 [8192, 28672], P('seq', 'tensor'), may hold values from -127 to 127, as said below
- down_codes: bfloat16 [28672, 8192], P('tensor', 'seq'), may hold values from -127 to 127, as said below
- gate_scale: int32 [28672], P('tensor'), may hold values from 1024 to 8191
- up_scale: int32 [28672], P('tensor'), may hold values from 1024 to 8191
- down_scale: int32 [8192], P('seq'), may hold values from 512 to 4095
- sign_bits: int32 [28672], P('tensor'), may hold values from 0 to 1
Outputs:
- ffn_output: bfloat16 [2048, 8192], P('tensor', 'seq')
Inputs may be any that keep to these rules, and one draw needn't show every extreme that they name: `gate_codes`: whole numbers. `up_codes`: whole numbers. `down_codes`: whole numbers.
All inputs are finite; a program needn't handle non-finite values.
Results may differ from a plain program's by a relative error of at most 0.039.
Values may be sent and summed in bfloat16 or wider, within the bound.
A program may use at most 128 MiB of HBM per device.

v0:
```python
import math

import jax
import jax.numpy as jnp
from jax import lax
from jax.sharding import PartitionSpec as P

BLOCK = 256


CODE_SCALE = 2.0 ** (-24)


def walsh_table(extent):
    row_ids = jnp.arange(extent, dtype=jnp.int32)[:, None]
    col_ids = jnp.arange(extent, dtype=jnp.int32)[None, :]
    common = jnp.bitwise_and(row_ids, col_ids)
    parity = jnp.zeros((extent, extent), jnp.int32)
    for bit_pos in range(max(extent.bit_length() - 1, 1)):
        parity = jnp.bitwise_xor(parity, jnp.bitwise_and(jnp.right_shift(common, bit_pos), 1))
    return (1 - 2 * parity).astype(jnp.float32)


def on_device(
    tokens, gate_codes, up_codes, down_codes, gate_scale, up_scale, down_scale, sign_bits
):
    gathered = lax.all_gather(tokens, "tensor", axis=0, tiled=True)
    gate_factor = gate_scale.astype(jnp.float32) * CODE_SCALE
    up_factor = up_scale.astype(jnp.float32) * CODE_SCALE
    hidden_width = gate_codes.shape[1]
    window = gathered
    gate_part = jnp.dot(window, gate_codes, preferred_element_type=jnp.float32) * gate_factor
    up_part = jnp.dot(window, up_codes, preferred_element_type=jnp.float32) * up_factor
    summed = lax.psum_scatter(
        jnp.concatenate([gate_part, up_part], axis=1).astype(jnp.bfloat16),
        "seq",
        scatter_dimension=0,
        tiled=True,
    ).astype(jnp.float32)
    hidden = (
        jax.nn.silu(summed[:, :hidden_width])
        * summed[:, hidden_width:]
        * (2 * sign_bits - 1).astype(jnp.float32)
    )
    local_rows = hidden.shape[0]
    blocks = hidden.reshape(local_rows, hidden_width // BLOCK, BLOCK)
    turned = jnp.einsum(
        "rbk,kj->rbj", blocks, walsh_table(BLOCK), precision=lax.Precision.HIGHEST
    ) * (1.0 / math.sqrt(BLOCK))
    rotated = turned.reshape(local_rows, hidden_width).astype(jnp.bfloat16)
    spread = lax.axis_size("tensor")
    norm_factor = 1.0 / math.sqrt(spread)
    walsh_small = walsh_table(spread)
    mixed_part = (
        jnp.einsum(
            "pq,qrc->prc",
            walsh_small,
            lax.all_to_all(rotated[None], "tensor", split_axis=2, concat_axis=0, tiled=True).astype(
                jnp.float32
            ),
            precision=lax.Precision.HIGHEST,
        )
        * norm_factor
    )
    outgoing = mixed_part.astype(jnp.bfloat16)
    returned = lax.all_to_all(outgoing, "tensor", split_axis=0, concat_axis=2, tiled=True)
    final_rows = returned.reshape(local_rows, hidden_width)
    everyone = lax.all_gather(final_rows, "seq", axis=0, tiled=True)
    down_factor = down_scale.astype(jnp.float32) * CODE_SCALE
    window = everyone
    return lax.psum_scatter(
        (jnp.dot(window, down_codes, preferred_element_type=jnp.float32) * down_factor).astype(
            jnp.bfloat16
        ),
        "tensor",
        scatter_dimension=0,
        tiled=True,
    )


def solution(mesh):
    placed = (
        P("tensor", "seq"),
        P("seq", "tensor"),
        P("seq", "tensor"),
        P("tensor", "seq"),
        P("tensor"),
        P("tensor"),
        P("seq"),
        P("tensor"),
    )
    return jax.shard_map(
        on_device, mesh=mesh, in_specs=placed, out_specs=P("tensor", "seq"), check_vma=False
    )
```

profile of v0, /device:TPU:2, one launch (start us, length us, event | category | flops | bytes accessed | tf_op | source)
XLA Modules:
  0.0 752.8 jit_solution(11592013410350668778)
XLA Ops:
  6.5 0.7 all-gather.3.cloned.1.call-update
  7.3 0.0 reduce-scatter.7.cloned.1.call-start
  7.3 0.7 convert_multiply_fusion
  8.0 0.7 convert_multiply_fusion.1
  8.7 57.6 %all-gather.3.cloned.1.call-done = bf16[2048,512]{1,0:T(8,128)(2,1)} async-done(((bf16[128,512]{1,0:T(8,128)(2,1)}), bf16[2048,512]{1,0:T(8,128)(2,1)}) %all-gather.3.cloned.1.call-update) | async-done | bytes 2097168 | tf_op jit(solution)/shard_map/all_gather | solution.py:27
  66.3 6.0 multiply_convert_fusion
  72.3 4.3 multiply_convert_fusion.1
  76.7 17.1 %pad_maximum_fusion = bf16[2048,3584]{0,1:T(8,128)(2,1)} fusion(bf16[2048,1792]{0,1:T(8,128)(2,1)S(1)} %multiply_convert_fusion, bf16[2048,1792]{0,1:T(8,128)(2,1)S(1)} %multiply_convert_fusion.1), kind=kLoop, calls=%fused_computation | loop fusion | flops 29360128 | bytes 29360128 | tf_op jit(solution)/shard_map/concatenate | solution.py:35
  93.8 18.8 %copy.20 = bf16[2048,3584]{1,0:T(8,128)(2,1)} copy(bf16[2048,3584]{0,1:T(8,128)(2,1)} %pad_maximum_fusion) | data formatting | bytes 29360128
  112.6 0.2 all-gather.5.cloned.1.call-start
  112.8 0.4 copy-done.2
  113.2 307.9 %reduce-scatter.7.cloned.1.call-done = bf16[128,3584]{1,0:T(8,128)(2,1)} async-done(((bf16[2048,3584]{1,0:T(8,128)(2,1)}), bf16[128,3584]{1,0:T(8,128)(2,1)}) %reduce-scatter.7.cloned.1.call-update) | async-done | bytes 917520
  421.1 1.5 copy.21
  422.7 0.1 convert_element_type.45
  422.8 0.3 fusion.2
  423.1 1.7 fusion.1
  424.9 0.3 copy.15
  425.1 7.1 copy.28
  432.3 0.5 broadcast.49
  432.8 10.2 %reduce = bf16[1792,128]{1,0:T(8,128)(2,1)S(1)} reduce(bf16[1792,1,128]{2,1,0:T(2,128)(2,1)S(1)} %bitcast.31, bf16[]{:T(256)} %broadcast.49), dimensions={1}, to_apply=%bitcast.30.reduce_sub_computation | reduce | bytes 917506
  443.0 0.1 reshape.29
  443.1 16.1 %all_to_all.33 = bf16[16,2,7168]{2,1,0:T(2,128)(2,1)S(1)} all-to-all(bf16[16,2,7168]{2,1,0:T(2,128)(2,1)S(1)} %reshape.29), channel_id=1, replica_groups=mesh['seq'=16,'tensor'=16] {'tensor'}, dimensions={0} | all-to-all | bytes 917504 | tf_op jit(solution)/shard_map/all_to_all | solution.py:58
  459.1 0.4 reshape.30
  459.5 0.1 copy.22
  459.6 0.5 fusion
  460.1 0.1 copy.18
  460.2 14.8 %all_to_all.34 = bf16[16,128,112]{1,2,0:T(8,128)(2,1)} all-to-all(bf16[16,128,112]{1,2,0:T(8,128)(2,1)S(1)} %copy.18), channel_id=1, replica_groups=mesh['seq'=16,'tensor'=16] {'tensor'}, dimensions={0} | all-to-all | bytes 917504 | tf_op jit(solution)/shard_map/all_to_all | solution.py:66
  475.1 0.0 all-gather.5.cloned.1.call-update
  475.1 0.3 reduce-scatter.5.cloned.1.call-start
  475.4 177.9 %all-gather.5.cloned.1.call-done = bf16[2048,1792]{0,1:T(8,128)(2,1)} async-done(((bf16[128,1792]{0,1:T(8,128)(2,1)}), bf16[2048,1792]{0,1:T(8,128)(2,1)}) %all-gather.5.cloned.1.call-update) | async-done | bytes 7340048 | tf_op jit(solution)/shard_map/all_gather | solution.py:68
  653.3 9.1 %multiply_convert_fusion.2 = bf16[2048,512]{1,0:T(8,128)(2,1)} fusion(bf16[2048,1792]{0,1:T(8,128)(2,1)} %all-gather.5.cloned.1.call-done, bf16[1792,512]{1,0:T(8,128)(2,1)} %param.11, f32[512]{0:T(512)S(1)} %convert_multiply_fusion.2), kind=kOutput, calls=%fused_computation.3 | convolution fusion | flops 3760193536 | bytes 11274240 | tf_op jit(solution)/shard_map/dot_general | solution.py:72
  662.5 83.8 %reduce-scatter.5.cloned.1.call-done = bf16[128,512]{1,0:T(8,128)(2,1)} async-done(((bf16[2048,512]{1,0:T(8,128)(2,1)}), bf16[128,512]{1,0:T(8,128)(2,1)}) %reduce-scatter.5.cloned.1.call-update) | async-done | bytes 131088 | tf_op jit(solution)/shard_map/reduce_scatter | solution.py:71
  (16 shorter events, 0.1 us)
Async XLA Ops:
  6.5 59.7 %copy-start = (bf16[512,1792]{1,0:T(8,128)(2,1)S(1)}, bf16[512,1792]{1,0:T(8,128)(2,1)}, u32[]{:S(2)}) copy-start(bf16[512,1792]{1,0:T(8,128)(2,1)} %param.10) | copy-start | bytes 5505028
  6.5 59.7 %all-gather.3.cloned.1.call-start = ((), (), s32[]{:S(2)}) async-start(), calls=%async_computation.4 | async-start | bytes 2228224 | tf_op jit(solution)/shard_map/all_gather | solution.py:27
  7.3 413.9 %reduce-scatter.7.cloned.1.call-start = ((), (), s32[]{:S(2)}) async-start(), calls=%async_computation.7 | async-start | bytes 15597568
  66.3 6.1 copy-start.4
  66.3 6.1 copy-start.5
  112.5 0.7 copy-start.2
  112.6 540.7 %all-gather.5.cloned.1.call-start = ((), (), s32[]{:S(2)}) async-start(), calls=%async_computation.5 | async-start | bytes 7798784 | tf_op jit(solution)/shard_map/all_gather | solution.py:68
  442.9 32.4 %copy-start.3 = (s32[512]{0:T(512)S(1)}, s32[512]{0:T(512)}, u32[]{:S(2)}) copy-start(s32[512]{0:T(512)} %param.14) | copy-start | bytes 6148
  475.1 271.2 %reduce-scatter.5.cloned.1.call-start = ((), (), s32[]{:S(2)}) async-start(), calls=%async_computation.6 | async-start | bytes 2228224 | tf_op jit(solution)/shard_map/reduce_scatter | solution.py:71
  653.3 93.0 %copy-start.1 = (bf16[512,1792]{1,0:T(8,128)(2,1)S(1)}, bf16[512,1792]{1,0:T(8,128)(2,1)}, u32[]{:S(2)}) copy-start(bf16[512,1792]{1,0:T(8,128)(2,1)} %param.10) | copy-start | bytes 5505028
Sparse Core Ops, SparseCore 0:
  10.0 56.1 all-gather.2
  112.7 308.3 reduce-scatter.6
  475.2 178.0 all-gather.4
  662.6 83.6 reduce-scatter.4
where the time goes:
time: 754 us; the launch traced here: 753 us
  waiting for transfers between devices  628 us (83%)
  blocking collectives  30.9 us (4%)
  local copies, waits for them, and re-layouts  29.3 us (4%)
  other arithmetic  29.1 us (4%)
  matrix products  21.7 us (3%)
  between operations  13.3 us (2%)
    unnamed x5, waiting for transfers between devices  309 us
    all_gather x1, waiting for transfers between devices, on_device(): everyone = lax.all_gather(final_rows, 'seq', axis=0, tiled=True)  178 us
    reduce_scatter x1, waiting for transfers between devices, on_device(): lax.psum_scatter((jnp.dot(window, down_codes, preferred_element_type=jnp....  83.8 us
    all_gather x1, waiting for transfers between devices, on_device(): gathered = lax.all_gather(tokens, 'tensor', axis=0, tiled=True)  57.6 us
    unnamed x18, local copies, waits for them, and re-layouts  21.8 us
    concatenate x1, other arithmetic, on_device(): jnp.concatenate([gate_part, up_part], axis=1).astype(jnp.bfloat16)  17.1 us
    all_to_all x1, blocking collectives, on_device(): lax.all_to_all(rotated[None], 'tensor', split_axis=2, concat_axis=0, tile...  16.1 us
  transfers between devices with their start and end apart: 4, of which 4 were waited for; matrix products, arithmetic and copies ran while one was open for 0% of the time, Pallas kernels for 0%

commit v1 on v0

v1 whole, which is shorter than its diff:
```python
import functools
import math

import jax
import jax.numpy as jnp
import numpy as np
from jax import lax
from jax.experimental import pallas as pl
from jax.experimental.pallas import tpu as pltpu
from jax.sharding import PartitionSpec as P

BLOCK = 256
TILE = 128
ROWS = 16
YL = 2
CORES = 2
CODE_SCALE = 2.0 ** (-24)
MESH = pl.DeviceIdType.MESH
F32 = jnp.float32
BF16 = jnp.bfloat16


def walsh(extent):
    ids = np.arange(extent)
    common = ids[:, None] & ids[None, :]
    parity = np.zeros_like(common)
    while common.any():
        parity ^= common & 1
        common = common >> 1
    return (1 - 2 * parity).astype(np.float32)


def kernel(
    cfg,
    tok_hbm, gate_hbm, up_hbm, down_hbm, fac_hbm, dfac_ref, walsh_ref,
    out_ref,
    tok, wv, dv, fac, part, ring, lr, ar, br, agr, dp, dr,
    tok_s, tok_r, wa, wb, w_s, wf_s, d_a, d_b, d_s, df_s, fac_r, fac_s,
    ring_s, ring_r, a_s, a_r, b_s, b_r, g_s, g_r, o_s, o_r,
):
    Z, K, NCH = cfg
    NP = K * YL
    half = Z // 2
    seq = lax.axis_index("seq")
    ten = lax.axis_index("tensor")
    z = seq // YL
    a = lax.rem(seq, YL)
    k = ten // CORES
    c = lax.rem(ten, CORES)
    me = k * YL + a
    diag = a == c

    def plane(p):
        return (z * YL + lax.rem(p, YL), (p // YL) * CORES + c)

    def ring_dev(d):
        step = 1 if d == 0 else Z - 1
        return (lax.rem(z + step, Z) * YL + a, ten)

    other_core = (seq, k * CORES + (1 - c))
    other_y = (z * YL + (1 - a), ten)

    def remote(src, dst, ss, rs, dev):
        return pltpu.make_async_remote_copy(
            src_ref=src, dst_ref=dst, send_sem=ss, recv_sem=rs,
            device_id=dev, device_id_type=MESH)

    barrier = pltpu.get_barrier_semaphore()

    def greet(i, _):
        pl.semaphore_signal(barrier, inc=1, device_id=plane(lax.rem(me + i, NP)), device_id_type=MESH)
        return 0

    lax.fori_loop(1, NP, greet, 0)
    pl.semaphore_signal(barrier, inc=1, device_id=other_core, device_id_type=MESH)
    for d in range(2):
        pl.semaphore_signal(barrier, inc=1, device_id=ring_dev(d), device_id_type=MESH)
    pl.semaphore_wait(barrier, NP - 1 + 3)

    def tok_copy(i):
        return remote(tok_hbm, tok.at[a, :, k], tok_s.at[i], tok_r.at[i], plane(lax.rem(me + i, NP)))

    def tok_start(i, _):
        tok_copy(i).start()
        return 0

    lax.fori_loop(1, NP, tok_start, 0)
    tok_own = pltpu.make_async_copy(tok_hbm, tok.at[a, :, k], tok_s.at[0])
    tok_own.start()

    def chunk_of(ref, ch):
        return ref.at[:, pl.ds(pl.multiple_of(ch * BLOCK, BLOCK), BLOCK)]

    def w_start(ch):
        for g, ref in enumerate((gate_hbm, up_hbm)):
            src = chunk_of(ref, ch)
            dst = wv.at[ch, a, g]

            @pl.when(diag)
            def _():
                pltpu.make_async_copy(src, dst, wa.at[ch]).start()
                remote(src, dst, w_s.at[ch], wa.at[ch], other_core).start()

            @pl.when(jnp.logical_not(diag))
            def _():
                remote(src, dst, w_s.at[ch], wb.at[ch], other_y).start()

    def w_wait(ch):
        pltpu.make_async_copy(wv.at[ch, a], wv.at[ch, a], wa.at[ch]).wait()
        pltpu.make_async_copy(wv.at[ch, 1 - a], wv.at[ch, 1 - a], wb.at[ch]).wait()

    def w_forward(ch):
        return remote(wv.at[ch, 1 - a], wv.at[ch, 1 - a], wf_s.at[ch], wb.at[ch], other_core)

    def d_start():
        for h in range(2):
            src = down_hbm.at[:, h]
            dst = dv.at[a, h]

            @pl.when(diag)
            def _():
                pltpu.make_async_copy(src, dst, d_a).start()
                remote(src, dst, d_s, d_a, other_core).start()

            @pl.when(jnp.logical_not(diag))
            def _():
                remote(src, dst, d_s, d_b, other_y).start()

    def d_forward():
        return remote(dv.at[1 - a], dv.at[1 - a], df_s, d_b, other_core)

    ahead = min(3, NCH)
    for ch in range(ahead):
        w_start(ch)

    @pl.when(diag)
    def _():
        pltpu.make_async_copy(fac_hbm, fac, fac_r).start()
        remote(fac_hbm, fac, fac_s, fac_r, other_core).start()

    pltpu.make_async_copy(fac, fac, fac_r).wait()

    def tok_wait(i, _):
        tok_copy(i).wait_recv()
        return 0

    lax.fori_loop(1, NP, tok_wait, 0)
    tok_own.wait()

    def ring_copy(d, ch, n):
        step = half - n if d == 0 else Z - half + n
        j = lax.rem(z + step, Z)
        if n == 0:
            return remote(part.at[ch, j, d], ring.at[d, ch, n, d], ring_s.at[d, ch, n], ring_r.at[d, ch, n], ring_dev(d))
        return remote(part.at[ch, j], ring.at[d, ch, n], ring_s.at[d, ch, n], ring_r.at[d, ch, n], ring_dev(d))

    def first(ch):
        w_wait(ch)

        @pl.when(diag)
        def _():
            w_forward(ch).start()

        def rows(m, _):
            for g in range(2):
                acc = jnp.zeros((2 * K * ROWS, BLOCK), F32)
                for f in range(2):
                    x = tok[f, pl.ds(2 * m, 2)].reshape(2 * K * ROWS, -1)
                    acc += jnp.dot(x, wv[ch, f, g], preferred_element_type=F32)
                part[ch, pl.ds(2 * m, 2), g] = acc.astype(BF16).reshape(2, K * ROWS, BLOCK)
            return 0

        lax.fori_loop(0, Z // 2, rows, 0)
        for d in range(2):
            ring_copy(d, ch, 0).start()

        @pl.when(ch + ahead < NCH)
        def _():
            w_start(ch + ahead)

        @pl.when(ch == NCH - 1)
        def _():
            d_start()

    def middle(ch, n):
        for d in range(2):
            ring_copy(d, ch, n - 1).wait_recv()
            step = half - n if d == 0 else Z - half + n
            j = lax.rem(z + step, Z)
            for g in ((d,) if n == 1 else (0, 1)):
                part[ch, j, g] = (part[ch, j, g].astype(F32) + ring[d, ch, n - 1, g].astype(F32)).astype(BF16)
            ring_copy(d, ch, n).start()

    def last(ch):
        n = half - 1
        for d in range(2):
            ring_copy(d, ch, n).wait_recv()
        sums = [
            part[ch, z, g].astype(F32) + ring[0, ch, n, g].astype(F32) + ring[1, ch, n, g].astype(F32)
            for g in range(2)
        ]
        table = fac[ch]
        gate = sums[0] * table[0:1]
        up = sums[1] * table[1:2]
        hidden = gate / (1.0 + jnp.exp(-gate)) * up * table[2:3]
        hi = hidden.astype(BF16)
        lo = (hidden - hi.astype(F32)).astype(BF16)
        w = walsh_ref[...]
        turned = jnp.dot(hi, w, preferred_element_type=F32) + jnp.dot(lo, w, preferred_element_type=F32)
        turned = (turned * (1.0 / math.sqrt(BLOCK))).astype(BF16)
        for h in range(2):
            lr[ch, h] = turned[:, h * TILE:(h + 1) * TILE].reshape(K, ROWS, TILE)

    def slot(t, _):
        for n in range(half, -1, -1):
            ch = t - n

            @pl.when(jnp.logical_and(ch >= 0, ch < NCH))
            def _():
                if n == 0:
                    first(ch)
                elif n == half:
                    last(ch)
                else:
                    middle(ch, n)

        return 0

    lax.fori_loop(0, NCH + half, slot, 0)

    my_r, my_h = me // 2, lax.rem(me, 2)

    def a_copy(i):
        p = lax.rem(me + i, NP)
        return remote(lr.at[:, lax.rem(p, 2), p // 2], ar.at[me], a_s.at[i], a_r.at[i], plane(p))

    def a_start(i, _):
        a_copy(i).start()
        return 0

    lax.fori_loop(1, NP, a_start, 0)
    ar[me] = lr[:, my_h, my_r]

    def a_wait(i, _):
        a_copy(i).wait_recv()
        return 0

    lax.fori_loop(1, NP, a_wait, 0)

    def mix(ch, _):
        vals = [ar[q, ch].astype(F32) for q in range(NP)]
        bit = 1
        while bit < NP:
            nxt = list(vals)
            for q in range(NP):
                if not q & bit:
                    nxt[q] = vals[q] + vals[q | bit]
                    nxt[q | bit] = vals[q] - vals[q | bit]
            vals = nxt
            bit *= 2
        for q in range(NP):
            br[q, :, pl.ds(pl.multiple_of(ch * TILE, TILE), TILE)] = (vals[q] * (1.0 / math.sqrt(NP))).astype(BF16)
        return 0

    lax.fori_loop(0, NCH, mix, 0)

    def b_copy(i):
        p = lax.rem(me + i, NP)
        return remote(br.at[p], agr.at[z, my_h, my_r], b_s.at[i], b_r.at[i], plane(p))

    def b_start(i, _):
        b_copy(i).start()
        return 0

    lax.fori_loop(1, NP, b_start, 0)
    agr[z, my_h, my_r] = br[me]

    pltpu.make_async_copy(dv.at[a], dv.at[a], d_a).wait()
    pltpu.make_async_copy(dv.at[1 - a], dv.at[1 - a], d_b).wait()

    @pl.when(diag)
    def _():
        d_forward().start()

    def b_wait(i, _):
        b_copy(i).wait_recv()
        return 0

    lax.fori_loop(1, NP, b_wait, 0)

    def g_copy(d, n, h):
        j = lax.rem(z + (Z - n if d == 0 else n), Z)
        return remote(agr.at[j, h], agr.at[j, h], g_s.at[d, n, h], g_r.at[d, n, h], ring_dev(d))

    def g_wait(d, n, h):
        j = lax.rem(z + (2 * Z - 1 - n if d == 0 else 1 + n), Z)
        pltpu.make_async_copy(agr.at[j, h], agr.at[j, h], g_r.at[d, n, h]).wait()

    def o_copy(j, i):
        p = lax.rem(me + i, NP)
        return remote(dp.at[j, lax.rem(p, 2), p // 2], dr.at[me, j], o_s.at[i], o_r.at[i], plane(p))

    def down(j):
        for f in range(2):
            for q in range(dp.shape[-1] // BLOCK):
                cols = slice(q * BLOCK, (q + 1) * BLOCK)
                acc = jnp.zeros((K * ROWS, BLOCK), F32)
                for h in range(2):
                    x = agr[j, h].reshape(K * ROWS, NCH * TILE)
                    acc += jnp.dot(x, dv[f, h, :, :, cols].reshape(NCH * TILE, BLOCK), preferred_element_type=F32)
                dp[j, f, :, :, cols] = acc.astype(BF16).reshape(K, ROWS, BLOCK)

        def o_start(i, _):
            o_copy(j, i).start()
            return 0

        lax.fori_loop(1, NP, o_start, 0)
        dr[me, j] = dp[j, a, k]

    for h in range(2):
        for d in range(2):
            if half > 1 or h == d:
                g_copy(d, 0, h).start()
    down(z)

    def around(n, _):
        for h in range(2):
            for d in range(2):
                g_wait(d, n, h)
                if h == d:
                    g_copy(d, n + 1, h).start()
                else:
                    @pl.when(n + 1 < half - 1)
                    def _():
                        g_copy(d, n + 1, h).start()

        down(lax.rem(z + Z - 1 - n, Z))
        down(lax.rem(z + 1 + n, Z))
        return 0

    lax.fori_loop(0, half - 1, around, 0)
    for d in range(2):
        g_wait(d, half - 1, d)
    down(lax.rem(z + half, Z))

    def o_wait(i, _):
        src = lax.rem(me + NP - i, NP)
        pltpu.make_async_copy(dr.at[src], dr.at[src], o_r.at[i]).wait()
        return 0

    lax.fori_loop(1, NP, o_wait, 0)

    def total(j, _):
        acc = dr[0, j].astype(F32)
        for q in range(1, NP):
            acc += dr[q, j].astype(F32)
        out_ref[pl.ds(pl.multiple_of(j * ROWS, ROWS), ROWS), :] = (acc * dfac_ref[...]).astype(BF16)
        return 0

    lax.fori_loop(0, Z, total, 0)

    def sent(i, _):
        tok_copy(i).wait_send()
        a_copy(i).wait_send()
        b_copy(i).wait_send()
        pltpu.make_async_copy(dr.at[0], dr.at[0], o_s.at[i]).wait()
        return 0

    lax.fori_loop(1, NP, sent, 0)

    def w_sent(ch, _):
        pltpu.make_async_copy(wv.at[ch, a], wv.at[ch, a], w_s.at[ch]).wait()

        @pl.when(diag)
        def _():
            w_forward(ch).wait_send()

        for d in range(2):
            for n in range(half):
                ring_copy(d, ch, n).wait_send()
        return 0

    lax.fori_loop(0, NCH, w_sent, 0)
    pltpu.make_async_copy(dv.at[a], dv.at[a], d_s).wait()

    @pl.when(diag)
    def _():
        d_forward().wait_send()
        remote(fac_hbm, fac, fac_s, fac_r, other_core).wait_send()

    for d in range(2):
        for n in range(half):
            for h in range(2):
                if n < half - 1 or h == d:
                    g_copy(d, n, h).wait_send()


def on_device(Z, K, tokens, gate_codes, up_codes, down_codes, gate_scale, up_scale, down_scale, sign_bits):
    feats = tokens.shape[1]
    width = gate_codes.shape[1]
    NCH = width // BLOCK
    NP = K * YL
    half = Z // 2
    table = jnp.stack(
        [
            gate_scale.astype(F32) * CODE_SCALE,
            up_scale.astype(F32) * CODE_SCALE,
            (2 * sign_bits - 1).astype(F32),
        ]
        + [jnp.zeros((width,), F32)] * 5
    )
    table = table.reshape(8, NCH, BLOCK).transpose(1, 0, 2)
    dfac = (down_scale.astype(F32) * CODE_SCALE)[None]
    dma = pltpu.SemaphoreType.DMA
    any_spec = pl.BlockSpec(memory_space=pl.ANY)
    vmem_spec = pl.BlockSpec(memory_space=pltpu.VMEM)
    return pl.pallas_call(
        functools.partial(kernel, (Z, K, NCH)),
        out_shape=jax.ShapeDtypeStruct(tokens.shape, BF16),
        in_specs=[any_spec] * 5 + [vmem_spec] * 2,
        out_specs=vmem_spec,
        scratch_shapes=[
            pltpu.VMEM((2, Z, K, ROWS, feats), BF16),
            pltpu.VMEM((NCH, 2, 2, feats, BLOCK), BF16),
            pltpu.VMEM((2, 2, NCH, TILE, feats), BF16),
            pltpu.VMEM((NCH, 8, BLOCK), F32),
            pltpu.VMEM((NCH, Z, 2, K * ROWS, BLOCK), BF16),
            pltpu.VMEM((2, NCH, half, 2, K * ROWS, BLOCK), BF16),
            pltpu.VMEM((NCH, 2, K, ROWS, TILE), BF16),
            pltpu.VMEM((NP, NCH, ROWS, TILE), BF16),
            pltpu.VMEM((NP, ROWS, NCH * TILE), BF16),
            pltpu.VMEM((Z, 2, K, ROWS, NCH * TILE), BF16),
            pltpu.VMEM((Z, 2, K, ROWS, feats), BF16),
            pltpu.VMEM((NP, Z, ROWS, feats), BF16),
            dma((NP,)), dma((NP,)),
            dma((NCH,)), dma((NCH,)), dma((NCH,)), dma((NCH,)),
            dma, dma, dma, dma,
            dma, dma,
            dma((2, NCH, half)), dma((2, NCH, half)),
            dma((NP,)), dma((NP,)), dma((NP,)), dma((NP,)),
            dma((2, half, 2)), dma((2, half, 2)),
            dma((NP,)), dma((NP,)),
        ],
        compiler_params=pltpu.CompilerParams(
            collective_id=0, has_side_effects=True, vmem_limit_bytes=56 * 1024 * 1024),
    )(
        tokens.reshape(Z, ROWS, feats),
        gate_codes,
        up_codes,
        down_codes.reshape(NCH, 2, TILE, down_codes.shape[1]),
        table,
        dfac,
        jnp.asarray(walsh(BLOCK), BF16),
    )


def solution(mesh):
    Z = mesh.shape["seq"] // YL
    K = mesh.shape["tensor"] // CORES
    placed = (
        P("tensor", "seq"),
        P("seq", "tensor"),
        P("seq", "tensor"),
        P("tensor", "seq"),
        P("tensor"),
        P("tensor"),
        P("seq"),
        P("tensor"),
    )
    return jax.shard_map(
        functools.partial(on_device, Z, K), mesh=mesh, in_specs=placed, out_specs=P("tensor", "seq"), check_vma=False
    )
```

time: 754 us -> 192 us (0.25)
  waiting for transfers between devices: 628 us -> 0 us
  Pallas kernels: 0 us -> 186 us
  blocking collectives: 30.9 us -> 0 us
  local copies, waits for them, and re-layouts: 29.3 us -> 2.3 us
  other arithmetic: 29.1 us -> 3.37 us
  matrix products: 21.7 us -> 0 us
  between operations: 13.3 us -> 0.02 us
    unnamed x5 -> x0, waiting for transfers between devices: 309 us -> none
    all_gather x2 -> x0, waiting for transfers between devices: 235 us -> none  [the longest x1 178 us: on_device(): everyone = lax.all_gather(final_rows, 'seq', axis=0, tiled=True)]
    pallas_call x0 -> x1, Pallas kernels: none -> 186 us  [on_device(): pl.pallas_call(functools.partial(kernel, (Z, K, NCH)), out_shape=jax.Shap...]
    reduce_scatter x1 -> x0, waiting for transfers between devices: 83.8 us -> none  [on_device(): lax.psum_scatter((jnp.dot(window, down_codes, preferred_element_type=jnp....]
    all_to_all x2 -> x0, blocking collectives: 30.9 us -> none  [the longest x1 16.1 us: on_device(): lax.all_to_all(rotated[None], 'tensor', split_axis=2, concat_axis=0, tile...]
    dot_general x5 -> x0, matrix products: 21.7 us -> none  [the longest x1 9.13 us: on_device(): jnp.dot(window, down_codes, preferred_element_type=jnp.float32)]
    unnamed x18 -> x1, local copies, waits for them, and re-layouts: 21.8 us -> 1.57 us
    concatenate x1 -> x0, other arithmetic: 17.1 us -> none  [on_device(): jnp.concatenate([gate_part, up_part], axis=1).astype(jnp.bfloat16)]
  transfers between devices with their start and end apart: 4 -> 0, of which waited for: 4 -> 0; matrix products, arithmetic and copies ran while one was open for 0% -> 0% of each run, Pallas kernels for 0% -> 0%
where the time goes in v1:
time: 192 us; the launch traced here: 191 us
  Pallas kernels  186 us (97%)
  other arithmetic  3.37 us (2%)
  local copies, waits for them, and re-layouts  2.3 us (1%)
    pallas_call x1, Pallas kernels, on_device(): pl.pallas_call(functools.partial(kernel, (Z, K, NCH)), out_shape=jax.Shap...  186 us

profile of v1, /device:TPU:2, one launch (start us, length us, event | category | flops | bytes accessed | tf_op | source)
XLA Modules:
  0.0 191.4 jit_solution(11188068672704694340)
XLA Ops:
  0.0 1.3 convert_multiply_fusion.2
  1.3 0.7 convert_multiply_fusion.1
  2.0 0.7 convert_multiply_fusion
  2.7 0.7 add_convert_fusion
  3.4 0.7 stack.19
  4.1 185.7 %shard_map.91 = bf16[128,512]{1,0:T(8,128)(2,1)} custom-call(bf16[8,16,512]{2,1,0:T(8,128)(2,1)} %bitcast.6, bf16[512,1792]{1,0:T(8,128)(2,1)} %gate_hbm.1, bf16[512,1792]{1,0:T(8,128)(2,1)} %up_hbm.1, bf16[7,2,128,512]{3,2,1,0:T(8,128)(2,1)} %bitcast.4, f32[7,8,256]{2,1,0:T(8,128)} %bitcast.5, f32[1,512]{1,0:T(1,128)} %bitcast.7, ...), custom_call_target="tpu_custom_call" | custom-call | tf_op jit(solution)/shard_map/pallas_call | solution.py:417
  189.8 1.6 copy.11
  (5 shorter events, 0.1 us)

commit v2 on v1

--- a/solution.py
+++ b/solution.py
@@ -13,6 +13,7 @@
 TILE = 128
 ROWS = 16
 YL = 2
+YH = 2
 CORES = 2
 CODE_SCALE = 2.0 ** (-24)
 MESH = pl.DeviceIdType.MESH
@@ -32,10 +33,10 @@
 
 def kernel(
     cfg,
-    tok_hbm, gate_hbm, up_hbm, down_hbm, fac_hbm, dfac_ref, walsh_ref,
+    tok_hbm, gate_hbm, up_hbm, down_hbm, gs_hbm, us_hbm, sb_hbm, ds_ref, walsh_ref,
     out_ref,
     tok, wv, dv, fac, part, ring, lr, ar, br, agr, dp, dr,
-    tok_s, tok_r, wa, wb, w_s, wf_s, d_a, d_b, d_s, df_s, fac_r, fac_s,
+    tok_s, tok_r, tok_o, wa, wb, w_s, wf_s, d_a, d_b, d_s, df_s, fac_r, fac_s,
     ring_s, ring_r, a_s, a_r, b_s, b_r, g_s, g_r, o_s, o_r,
 ):
     Z, K, NCH = cfg
@@ -65,28 +66,110 @@
             src_ref=src, dst_ref=dst, send_sem=ss, recv_sem=rs,
             device_id=dev, device_id_type=MESH)
 
+    NY = YH * YL
+    NX = NP // NY
+    x, y = k // YH, lax.rem(k, YH) * YL + a
+
+    def chip(cx, cy):
+        return (z * YL + lax.rem(cy, YL), (cx * YH + cy // YL) * CORES + c)
+
+    def moved(axis, by):
+        if axis == 0:
+            return lax.rem(x + by, NX), y
+        return x, lax.rem(y + by, NY)
+
     barrier = pltpu.get_barrier_semaphore()
-
-    def greet(i, _):
-        pl.semaphore_signal(barrier, inc=1, device_id=plane(lax.rem(me + i, NP)), device_id_type=MESH)
-        return 0
-
-    lax.fori_loop(1, NP, greet, 0)
-    pl.semaphore_signal(barrier, inc=1, device_id=other_core, device_id_type=MESH)
-    for d in range(2):
-        pl.semaphore_signal(barrier, inc=1, device_id=ring_dev(d), device_id_type=MESH)
-    pl.semaphore_wait(barrier, NP - 1 + 3)
-
-    def tok_copy(i):
-        return remote(tok_hbm, tok.at[a, :, k], tok_s.at[i], tok_r.at[i], plane(lax.rem(me + i, NP)))
-
-    def tok_start(i, _):
-        tok_copy(i).start()
-        return 0
-
-    lax.fori_loop(1, NP, tok_start, 0)
-    tok_own = pltpu.make_async_copy(tok_hbm, tok.at[a, :, k], tok_s.at[0])
-    tok_own.start()
+    near = [chip(*moved(0, 1)), chip(*moved(0, NX - 1)), chip(*moved(1, 1)), chip(*moved(1, NY - 1)),
+            other_core, ring_dev(0), ring_dev(1)]
+    for dev in near:
+        pl.semaphore_signal(barrier, inc=1, device_id=dev, device_id_type=MESH)
+    pl.semaphore_wait(barrier, len(near))
+
+    feats = tok.shape[-1]
+    wide = feats // 2
+    tok_own = pltpu.make_async_copy(tok_hbm, tok.at[a, :, k], tok_o)
+
+    def spot(f, cx, cy, rows=slice(None)):
+        return tok.at[lax.rem(cy, YL), rows, cx * YH + cy // YL, :, f * wide:(f + 1) * wide]
+
+    def tok_copy(f, stage, i, d, hop):
+        axis = f if stage == 0 else 1 - f
+        size = NX if axis == 0 else NY
+        by = 1 if d == 0 else size - 1
+        dev = chip(*moved(axis, by))
+        back = size - 1 if d == 0 else 1
+        cx, cy = moved(axis, back) if hop else (x, y)
+        if stage == 1:
+            if f == 0:
+                cx = lax.rem(x + i, NX)
+            else:
+                cy = lax.rem(y + i, NY)
+        rows = slice(None) if not hop else (slice(0, Z // 2) if d == 0 else slice(Z // 2, Z))
+        sem = (f, 1 + i if stage == 1 else 0, d, hop)
+        dst = spot(f, cx, cy, rows)
+        src = tok_hbm.at[:, :, f * wide:(f + 1) * wide] if stage == 0 and not hop else dst
+        if stage == 1 and not hop and i == 0:
+            src = tok_hbm.at[:, :, f * wide:(f + 1) * wide]
+        return remote(src, dst, tok_s.at[sem], tok_r.at[sem], dev)
+
+    def tok_arrived(f, stage, i, d, hop):
+        axis = f if stage == 0 else 1 - f
+        size = NX if axis == 0 else NY
+        n = 2 if hop else 1
+        by = size - n if d == 0 else n
+        cx, cy = moved(axis, by)
+        if stage == 1:
+            if f == 0:
+                cx = lax.rem(x + i, NX)
+            else:
+                cy = lax.rem(y + i, NY)
+        rows = slice(None) if not hop else (slice(0, Z // 2) if d == 0 else slice(Z // 2, Z))
+        sem = (f, 1 + i if stage == 1 else 0, d, hop)
+        ref = spot(f, cx, cy, rows)
+        pltpu.make_async_copy(ref, ref, tok_r.at[sem]).wait()
+
+    def tok_begin():
+        for f in range(2):
+            for d in range(2):
+                tok_copy(f, 0, 0, d, 0).start()
+        tok_own.start()
+        for f in range(2):
+            for d in range(2):
+                tok_copy(f, 1, 0, d, 0).start()
+
+    def tok_relay():
+        for d in range(2):
+            for f in range(2):
+                tok_arrived(f, 0, 0, d, 0)
+                tok_copy(f, 0, 0, d, 1).start()
+                i = 3 if d == 0 else 1
+                for e in range(2):
+                    tok_copy(f, 1, i, e, 0).start()
+        for f in range(2):
+            for d in range(2):
+                tok_arrived(f, 0, 0, d, 1)
+            for e in range(2):
+                tok_copy(f, 1, 2, e, 0).start()
+        for i in (0, 3, 1, 2):
+            for f in range(2):
+                for d in range(2):
+                    tok_arrived(f, 1, i, d, 0)
+                    tok_copy(f, 1, i, d, 1).start()
+        for i in (0, 3, 1, 2):
+            for f in range(2):
+                for d in range(2):
+                    tok_arrived(f, 1, i, d, 1)
+        tok_own.wait()
+
+    def tok_sent():
+        for f in range(2):
+            for d in range(2):
+                for hop in range(2):
+                    tok_copy(f, 0, 0, d, hop).wait_send()
+                    for i in range(4):
+                        tok_copy(f, 1, i, d, hop).wait_send()
+
+    tok_begin()
 
     def chunk_of(ref, ch):
         return ref.at[:, pl.ds(pl.multiple_of(ch * BLOCK, BLOCK), BLOCK)]
@@ -135,17 +218,13 @@
 
     @pl.when(diag)
     def _():
-        pltpu.make_async_copy(fac_hbm, fac, fac_r).start()
-        remote(fac_hbm, fac, fac_s, fac_r, other_core).start()
-
-    pltpu.make_async_copy(fac, fac, fac_r).wait()
-
-    def tok_wait(i, _):
-        tok_copy(i).wait_recv()
-        return 0
-
-    lax.fori_loop(1, NP, tok_wait, 0)
-    tok_own.wait()
+        for i, ref in enumerate((gs_hbm, us_hbm, sb_hbm)):
+            pltpu.make_async_copy(ref, fac.at[i], fac_r.at[i]).start()
+            remote(ref, fac.at[i], fac_s.at[i], fac_r.at[i], other_core).start()
+
+    tok_relay()
+    for i in range(3):
+        pltpu.make_async_copy(fac.at[i], fac.at[i], fac_r.at[i]).wait()
 
     def ring_copy(d, ch, n):
         step = half - n if d == 0 else Z - half + n
@@ -199,10 +278,12 @@
             part[ch, z, g].astype(F32) + ring[0, ch, n, g].astype(F32) + ring[1, ch, n, g].astype(F32)
             for g in range(2)
         ]
-        table = fac[ch]
-        gate = sums[0] * table[0:1]
-        up = sums[1] * table[1:2]
-        hidden = gate / (1.0 + jnp.exp(-gate)) * up * table[2:3]
+        gate_f, up_f, sign = [
+            jnp.concatenate([fac[i, pl.ds(2 * ch + h, 1), :] for h in range(2)], axis=1) for i in range(3)
+        ]
+        gate = sums[0] * (gate_f.astype(F32) * CODE_SCALE)
+        up = sums[1] * (up_f.astype(F32) * CODE_SCALE)
+        hidden = gate / (1.0 + jnp.exp(-gate)) * up * (2 * sign - 1).astype(F32)
         hi = hidden.astype(BF16)
         lo = (hidden - hi.astype(F32)).astype(BF16)
         w = walsh_ref[...]
@@ -350,23 +431,25 @@
 
     lax.fori_loop(1, NP, o_wait, 0)
 
+    down_f = jnp.concatenate([ds_ref[i:i + 1, :] for i in range(ds_ref.shape[0])], axis=1).astype(F32) * CODE_SCALE
+
     def total(j, _):
         acc = dr[0, j].astype(F32)
         for q in range(1, NP):
             acc += dr[q, j].astype(F32)
-        out_ref[pl.ds(pl.multiple_of(j * ROWS, ROWS), ROWS), :] = (acc * dfac_ref[...]).astype(BF16)
+        out_ref[pl.ds(pl.multiple_of(j * ROWS, ROWS), ROWS), :] = (acc * down_f).astype(BF16)
         return 0
 
     lax.fori_loop(0, Z, total, 0)
 
     def sent(i, _):
-        tok_copy(i).wait_send()
         a_copy(i).wait_send()
         b_copy(i).wait_send()
         pltpu.make_async_copy(dr.at[0], dr.at[0], o_s.at[i]).wait()
         return 0
 
     lax.fori_loop(1, NP, sent, 0)
+    tok_sent()
 
     def w_sent(ch, _):
         pltpu.make_async_copy(wv.at[ch, a], wv.at[ch, a], w_s.at[ch]).wait()
@@ -386,7 +469,8 @@
     @pl.when(diag)
     def _():
         d_forward().wait_send()
-        remote(fac_hbm, fac, fac_s, fac_r, other_core).wait_send()
+        for i, ref in enumerate((gs_hbm, us_hbm, sb_hbm)):
+            remote(ref, fac.at[i], fac_s.at[i], fac_r.at[i], other_core).wait_send()
 
     for d in range(2):
         for n in range(half):
@@ -401,29 +485,19 @@
     NCH = width // BLOCK
     NP = K * YL
     half = Z // 2
-    table = jnp.stack(
-        [
-            gate_scale.astype(F32) * CODE_SCALE,
-            up_scale.astype(F32) * CODE_SCALE,
-            (2 * sign_bits - 1).astype(F32),
-        ]
-        + [jnp.zeros((width,), F32)] * 5
-    )
-    table = table.reshape(8, NCH, BLOCK).transpose(1, 0, 2)
-    dfac = (down_scale.astype(F32) * CODE_SCALE)[None]
     dma = pltpu.SemaphoreType.DMA
     any_spec = pl.BlockSpec(memory_space=pl.ANY)
     vmem_spec = pl.BlockSpec(memory_space=pltpu.VMEM)
     return pl.pallas_call(
         functools.partial(kernel, (Z, K, NCH)),
         out_shape=jax.ShapeDtypeStruct(tokens.shape, BF16),
-        in_specs=[any_spec] * 5 + [vmem_spec] * 2,
+        in_specs=[any_spec] * 7 + [vmem_spec] * 2,
         out_specs=vmem_spec,
         scratch_shapes=[
             pltpu.VMEM((2, Z, K, ROWS, feats), BF16),
             pltpu.VMEM((NCH, 2, 2, feats, BLOCK), BF16),
             pltpu.VMEM((2, 2, NCH, TILE, feats), BF16),
-            pltpu.VMEM((NCH, 8, BLOCK), F32),
+            pltpu.VMEM((3, 2 * NCH, TILE), jnp.int32),
             pltpu.VMEM((NCH, Z, 2, K * ROWS, BLOCK), BF16),
             pltpu.VMEM((2, NCH, half, 2, K * ROWS, BLOCK), BF16),
             pltpu.VMEM((NCH, 2, K, ROWS, TILE), BF16),
@@ -432,10 +506,10 @@
             pltpu.VMEM((Z, 2, K, ROWS, NCH * TILE), BF16),
             pltpu.VMEM((Z, 2, K, ROWS, feats), BF16),
             pltpu.VMEM((NP, Z, ROWS, feats), BF16),
-            dma((NP,)), dma((NP,)),
+            dma((2, 5, 2, 2)), dma((2, 5, 2, 2)), dma,
             dma((NCH,)), dma((NCH,)), dma((NCH,)), dma((NCH,)),
             dma, dma, dma, dma,
-            dma, dma,
+            dma((3,)), dma((3,)),
             dma((2, NCH, half)), dma((2, NCH, half)),
             dma((NP,)), dma((NP,)), dma((NP,)), dma((NP,)),
             dma((2, half, 2)), dma((2, half, 2)),
@@ -448,8 +522,10 @@
         gate_codes,
         up_codes,
         down_codes.reshape(NCH, 2, TILE, down_codes.shape[1]),
-        table,
-        dfac,
+        gate_scale.reshape(2 * NCH, TILE),
+        up_scale.reshape(2 * NCH, TILE),
+        sign_bits.reshape(2 * NCH, TILE),
+        down_scale.reshape(feats // TILE, TILE),
         jnp.asarray(walsh(BLOCK), BF16),
     )
 

time: 192 us -> 185 us (0.964)
  other arithmetic: 3.37 us -> 0 us
  Pallas kernels: 186 us -> 183 us
    pallas_call x1, Pallas kernels: 186 us -> 183 us  [on_device(): pl.pallas_call(functools.partial(kernel, (Z, K, NCH)), out_shape=jax.Shap...]
    mul x3 -> x0, other arithmetic: 2.67 us -> none  [the longest x1 1.27 us: on_device(): dfac = (down_scale.astype(F32) * CODE_SCALE)[None]]
where the time goes in v2:
time: 185 us; the launch traced here: 184 us
  Pallas kernels  183 us (99%)
    pallas_call x1, Pallas kernels, on_device(): pl.pallas_call(functools.partial(kernel, (Z, K, NCH)), out_shape=jax.Shap...  183 us

profile of v2, /device:TPU:2, one launch (start us, length us, event | category | flops | bytes accessed | tf_op | source)
XLA Modules:
  0.0 184.2 jit_solution(14141590081134229095)
XLA Ops:
  0.0 182.6 %shard_map.91 = bf16[128,512]{1,0:T(8,128)(2,1)} custom-call(bf16[8,16,512]{2,1,0:T(8,128)(2,1)} %bitcast.7, bf16[512,1792]{1,0:T(8,128)(2,1)} %gate_hbm.1, bf16[512,1792]{1,0:T(8,128)(2,1)} %up_hbm.1, bf16[7,2,128,512]{3,2,1,0:T(8,128)(2,1)} %bitcast.6, s32[14,128]{1,0:T(8,128)} %bitcast.8, s32[14,128]{1,0:T(8,128)} %bitcast.9, s32[14,128]{1,0:T(8,128)} %bitcast.10, ...), custom_call_target="tpu_custom_call" | custom-call | tf_op jit(solution)/shard_map/pallas_call | solution.py:491
  182.6 1.6 copy.11

commit v3 on v2

--- a/solution.py
+++ b/solution.py
@@ -196,25 +196,20 @@
         return remote(wv.at[ch, 1 - a], wv.at[ch, 1 - a], wf_s.at[ch], wb.at[ch], other_core)
 
     def d_start():
-        for h in range(2):
-            src = down_hbm.at[:, h]
-            dst = dv.at[a, h]
-
-            @pl.when(diag)
-            def _():
-                pltpu.make_async_copy(src, dst, d_a).start()
-                remote(src, dst, d_s, d_a, other_core).start()
-
-            @pl.when(jnp.logical_not(diag))
-            def _():
-                remote(src, dst, d_s, d_b, other_y).start()
+        @pl.when(diag)
+        def _():
+            pltpu.make_async_copy(down_hbm, dv.at[a], d_a).start()
+            remote(down_hbm, dv.at[a], d_s, d_a, other_core).start()
+
+        @pl.when(jnp.logical_not(diag))
+        def _():
+            remote(down_hbm, dv.at[a], d_s, d_b, other_y).start()
 
     def d_forward():
         return remote(dv.at[1 - a], dv.at[1 - a], df_s, d_b, other_core)
 
     ahead = min(3, NCH)
-    for ch in range(ahead):
-        w_start(ch)
+    w_start(0)
 
     @pl.when(diag)
     def _():
@@ -223,6 +218,8 @@
             remote(ref, fac.at[i], fac_s.at[i], fac_r.at[i], other_core).start()
 
     tok_relay()
+    for ch in range(1, ahead):
+        w_start(ch)
     for i in range(3):
         pltpu.make_async_copy(fac.at[i], fac.at[i], fac_r.at[i]).wait()
 
@@ -233,7 +230,7 @@
             return remote(part.at[ch, j, d], ring.at[d, ch, n, d], ring_s.at[d, ch, n], ring_r.at[d, ch, n], ring_dev(d))
         return remote(part.at[ch, j], ring.at[d, ch, n], ring_s.at[d, ch, n], ring_r.at[d, ch, n], ring_dev(d))
 
-    def first(ch):
+    def product(ch):
         w_wait(ch)
 
         @pl.when(diag)
@@ -250,8 +247,6 @@
             return 0
 
         lax.fori_loop(0, Z // 2, rows, 0)
-        for d in range(2):
-            ring_copy(d, ch, 0).start()
 
         @pl.when(ch + ahead < NCH)
         def _():
@@ -292,44 +287,33 @@
         for h in range(2):
             lr[ch, h] = turned[:, h * TILE:(h + 1) * TILE].reshape(K, ROWS, TILE)
 
-    def slot(t, _):
-        for n in range(half, -1, -1):
-            ch = t - n
-
-            @pl.when(jnp.logical_and(ch >= 0, ch < NCH))
-            def _():
-                if n == 0:
-                    first(ch)
-                elif n == half:
-                    last(ch)
-                else:
-                    middle(ch, n)
-
-        return 0
-
-    lax.fori_loop(0, NCH + half, slot, 0)
-
     my_r, my_h = me // 2, lax.rem(me, 2)
 
-    def a_copy(i):
+    def a_copy(ch, i):
         p = lax.rem(me + i, NP)
-        return remote(lr.at[:, lax.rem(p, 2), p // 2], ar.at[me], a_s.at[i], a_r.at[i], plane(p))
-
-    def a_start(i, _):
-        a_copy(i).start()
-        return 0
-
-    lax.fori_loop(1, NP, a_start, 0)
-    ar[me] = lr[:, my_h, my_r]
-
-    def a_wait(i, _):
-        a_copy(i).wait_recv()
-        return 0
-
-    lax.fori_loop(1, NP, a_wait, 0)
-
-    def mix(ch, _):
-        vals = [ar[q, ch].astype(F32) for q in range(NP)]
+        return remote(lr.at[ch, lax.rem(p, 2), p // 2], ar.at[ch, me], a_s.at[ch], a_r.at[ch], plane(p))
+
+    def b_copy(ch, i):
+        p = lax.rem(me + i, NP)
+        return remote(br.at[ch, p], agr.at[z, ch, my_h, my_r], b_s.at[ch], b_r.at[ch], plane(p))
+
+    def others(copy, ch):
+        def start(i, _):
+            copy(ch, i).start()
+            return 0
+
+        lax.fori_loop(1, NP, start, 0)
+
+    def all_others(sem):
+        pltpu.make_async_copy(ar.at[0, 1:NP], ar.at[0, 1:NP], sem).wait()
+
+    def a_send(ch):
+        others(a_copy, ch)
+        ar[ch, me] = lr[ch, my_h, my_r]
+
+    def mix(ch):
+        all_others(a_r.at[ch])
+        vals = [ar[ch, q].astype(F32) for q in range(NP)]
         bit = 1
         while bit < NP:
             nxt = list(vals)
@@ -340,55 +324,41 @@
             vals = nxt
             bit *= 2
         for q in range(NP):
-            br[q, :, pl.ds(pl.multiple_of(ch * TILE, TILE), TILE)] = (vals[q] * (1.0 / math.sqrt(NP))).astype(BF16)
-        return 0
-
-    lax.fori_loop(0, NCH, mix, 0)
-
-    def b_copy(i):
-        p = lax.rem(me + i, NP)
-        return remote(br.at[p], agr.at[z, my_h, my_r], b_s.at[i], b_r.at[i], plane(p))
-
-    def b_start(i, _):
-        b_copy(i).start()
-        return 0
-
-    lax.fori_loop(1, NP, b_start, 0)
-    agr[z, my_h, my_r] = br[me]
-
-    pltpu.make_async_copy(dv.at[a], dv.at[a], d_a).wait()
-    pltpu.make_async_copy(dv.at[1 - a], dv.at[1 - a], d_b).wait()
-
-    @pl.when(diag)
-    def _():
-        d_forward().start()
-
-    def b_wait(i, _):
-        b_copy(i).wait_recv()
-        return 0
-
-    lax.fori_loop(1, NP, b_wait, 0)
-
-    def g_copy(d, n, h):
+            br[ch, q] = (vals[q] * (1.0 / math.sqrt(NP))).astype(BF16)
+        others(b_copy, ch)
+        agr[z, ch, my_h, my_r] = br[ch, me]
+
+    def g_copy(d, ch, n):
         j = lax.rem(z + (Z - n if d == 0 else n), Z)
-        return remote(agr.at[j, h], agr.at[j, h], g_s.at[d, n, h], g_r.at[d, n, h], ring_dev(d))
-
-    def g_wait(d, n, h):
+        ref = agr.at[j, ch] if n < half - 1 else agr.at[j, ch, d]
+        return remote(ref, ref, g_s.at[d, ch, n], g_r.at[d, ch, n], ring_dev(d))
+
+    def g_wait(d, ch, n):
         j = lax.rem(z + (2 * Z - 1 - n if d == 0 else 1 + n), Z)
-        pltpu.make_async_copy(agr.at[j, h], agr.at[j, h], g_r.at[d, n, h]).wait()
+        ref = agr.at[j, ch] if n < half - 1 else agr.at[j, ch, d]
+        pltpu.make_async_copy(ref, ref, g_r.at[d, ch, n]).wait()
+
+    def g_send(ch, n):
+        for d in range(2):
+            g_copy(d, ch, n).start()
+
+    def g_take(ch, n):
+        for d in range(2):
+            g_wait(d, ch, n)
+            if n + 1 < half:
+                g_copy(d, ch, n + 1).start()
 
     def o_copy(j, i):
         p = lax.rem(me + i, NP)
         return remote(dp.at[j, lax.rem(p, 2), p // 2], dr.at[me, j], o_s.at[i], o_r.at[i], plane(p))
 
     def down(j):
+        x = jnp.concatenate(
+            [agr[j, ch, h].reshape(K * ROWS, TILE) for ch in range(NCH) for h in range(2)], axis=1)
         for f in range(2):
-            for q in range(dp.shape[-1] // BLOCK):
+            for q in range(feats // BLOCK):
                 cols = slice(q * BLOCK, (q + 1) * BLOCK)
-                acc = jnp.zeros((K * ROWS, BLOCK), F32)
-                for h in range(2):
-                    x = agr[j, h].reshape(K * ROWS, NCH * TILE)
-                    acc += jnp.dot(x, dv[f, h, :, :, cols].reshape(NCH * TILE, BLOCK), preferred_element_type=F32)
+                acc = jnp.dot(x, dv[f, :, :, :, cols].reshape(NCH * BLOCK, BLOCK), preferred_element_type=F32)
                 dp[j, f, :, :, cols] = acc.astype(BF16).reshape(K, ROWS, BLOCK)
 
         def o_start(i, _):
@@ -398,31 +368,62 @@
         lax.fori_loop(1, NP, o_start, 0)
         dr[me, j] = dp[j, a, k]
 
-    for h in range(2):
-        for d in range(2):
-            if half > 1 or h == d:
-                g_copy(d, 0, h).start()
-    down(z)
-
-    def around(n, _):
-        for h in range(2):
+    def down_near(n):
+        def one(i, _):
+            down(lax.rem(z + jnp.where(i == 0, Z - 1 - n, 1 + n), Z))
+            return 0
+
+        lax.fori_loop(0, 2 if n < half - 1 else 1, one, 0)
+
+    def slot(t, _):
+        def at(n, do):
+            ch = t - n
+
+            @pl.when(jnp.logical_and(ch >= 0, ch < NCH))
+            def _():
+                do(ch)
+
+        def ring_first(ch):
             for d in range(2):
-                g_wait(d, n, h)
-                if h == d:
-                    g_copy(d, n + 1, h).start()
-                else:
-                    @pl.when(n + 1 < half - 1)
-                    def _():
-                        g_copy(d, n + 1, h).start()
-
-        down(lax.rem(z + Z - 1 - n, Z))
-        down(lax.rem(z + 1 + n, Z))
+                ring_copy(d, ch, 0).start()
+
+        def back(ch):
+            all_others(b_r.at[ch])
+            g_send(ch, 0)
+
+        at(0, ring_first)
+        for n in range(half - 1, 0, -1):
+            at(n, functools.partial(middle, n=n))
+        for n in range(half - 1, -1, -1):
+            at(half + 3 + n, functools.partial(g_take, n=n))
+        at(half + 2, back)
+        at(half + 1, mix)
+        at(half, last)
+        at(half, a_send)
+        at(-1, product)
+
+        @pl.when(t == NCH + half - 1)
+        def _():
+            pltpu.make_async_copy(dv.at[a], dv.at[a], d_a).wait()
+            pltpu.make_async_copy(dv.at[1 - a], dv.at[1 - a], d_b).wait()
+
+            @pl.when(diag)
+            def _():
+                d_forward().start()
+
+        @pl.when(t == NCH - 1 + half + 2)
+        def _():
+            down(z)
+
+        for n in range(half):
+            @pl.when(t == NCH - 1 + half + 3 + n)
+            def _():
+                down_near(n)
+
         return 0
 
-    lax.fori_loop(0, half - 1, around, 0)
-    for d in range(2):
-        g_wait(d, half - 1, d)
-    down(lax.rem(z + half, Z))
+    product(0)
+    lax.fori_loop(0, NCH + 2 * half + 2, slot, 0)
 
     def o_wait(i, _):
         src = lax.rem(me + NP - i, NP)
@@ -443,8 +444,6 @@
     lax.fori_loop(0, Z, total, 0)
 
     def sent(i, _):
-        a_copy(i).wait_send()
-        b_copy(i).wait_send()
         pltpu.make_async_copy(dr.at[0], dr.at[0], o_s.at[i]).wait()
         return 0
 
@@ -461,6 +460,9 @@
         for d in range(2):
             for n in range(half):
                 ring_copy(d, ch, n).wait_send()
+                g_copy(d, ch, n).wait_send()
+        all_others(a_s.at[ch])
+        all_others(b_s.at[ch])
         return 0
 
     lax.fori_loop(0, NCH, w_sent, 0)
@@ -471,12 +473,6 @@
         d_forward().wait_send()
         for i, ref in enumerate((gs_hbm, us_hbm, sb_hbm)):
             remote(ref, fac.at[i], fac_s.at[i], fac_r.at[i], other_core).wait_send()
-
-    for d in range(2):
-        for n in range(half):
-            for h in range(2):
-                if n < half - 1 or h == d:
-                    g_copy(d, n, h).wait_send()
 
 
 def on_device(Z, K, tokens, gate_codes, up_codes, down_codes, gate_scale, up_scale, down_scale, sign_bits):
@@ -496,14 +492,14 @@
         scratch_shapes=[
             pltpu.VMEM((2, Z, K, ROWS, feats), BF16),
             pltpu.VMEM((NCH, 2, 2, feats, BLOCK), BF16),
-            pltpu.VMEM((2, 2, NCH, TILE, feats), BF16),
+            pltpu.VMEM((2, NCH, 2, TILE, feats), BF16),
             pltpu.VMEM((3, 2 * NCH, TILE), jnp.int32),
             pltpu.VMEM((NCH, Z, 2, K * ROWS, BLOCK), BF16),
             pltpu.VMEM((2, NCH, half, 2, K * ROWS, BLOCK), BF16),
             pltpu.VMEM((NCH, 2, K, ROWS, TILE), BF16),
-            pltpu.VMEM((NP, NCH, ROWS, TILE), BF16),
-            pltpu.VMEM((NP, ROWS, NCH * TILE), BF16),
-            pltpu.VMEM((Z, 2, K, ROWS, NCH * TILE), BF16),
+            pltpu.VMEM((NCH, NP, ROWS, TILE), BF16),
+            pltpu.VMEM((NCH, NP, ROWS, TILE), BF16),
+            pltpu.VMEM((Z, NCH, 2, K, ROWS, TILE), BF16),
             pltpu.VMEM((Z, 2, K, ROWS, feats), BF16),
             pltpu.VMEM((NP, Z, ROWS, feats), BF16),
             dma((2, 5, 2, 2)), dma((2, 5, 2, 2)), dma,
@@ -511,8 +507,8 @@
             dma, dma, dma, dma,
             dma((3,)), dma((3,)),
             dma((2, NCH, half)), dma((2, NCH, half)),
-            dma((NP,)), dma((NP,)), dma((NP,)), dma((NP,)),
-            dma((2, half, 2)), dma((2, half, 2)),
+            dma((NCH,)), dma((NCH,)), dma((NCH,)), dma((NCH,)),
+            dma((2, NCH, half)), dma((2, NCH, half)),
             dma((NP,)), dma((NP,)),
         ],
         compiler_params=pltpu.CompilerParams(

time: 185 us -> 169 us (0.914)
  Pallas kernels: 183 us -> 165 us
    pallas_call x1, Pallas kernels: 183 us -> 165 us  [on_device(): pl.pallas_call(functools.partial(kernel, (Z, K, NCH)), out_shape=jax.Shap...]
where the time goes in v3:
time: 169 us; the launch traced here: 167 us
  Pallas kernels  165 us (98%)
    pallas_call x1, Pallas kernels, on_device(): pl.pallas_call(functools.partial(kernel, (Z, K, NCH)), out_shape=jax.Shap...  165 us

profile of v3, /device:TPU:2, one launch (start us, length us, event | category | flops | bytes accessed | tf_op | source)
XLA Modules:
  0.0 166.6 jit_solution(5104430576962329815)
XLA Ops:
  0.0 165.0 %shard_map.91 = bf16[128,512]{1,0:T(8,128)(2,1)} custom-call(bf16[8,16,512]{2,1,0:T(8,128)(2,1)} %bitcast.7, bf16[512,1792]{1,0:T(8,128)(2,1)} %gate_hbm.1, bf16[512,1792]{1,0:T(8,128)(2,1)} %up_hbm.1, bf16[7,2,128,512]{3,2,1,0:T(8,128)(2,1)} %bitcast.6, s32[14,128]{1,0:T(8,128)} %bitcast.8, s32[14,128]{1,0:T(8,128)} %bitcast.9, s32[14,128]{1,0:T(8,128)} %bitcast.10, ...), custom_call_target="tpu_custom_call" | custom-call | tf_op jit(solution)/shard_map/pallas_call | solution.py:487
  165.0 1.6 copy.11

commit v4 on v3

--- a/solution.py
+++ b/solution.py
@@ -3,7 +3,6 @@
 
 import jax
 import jax.numpy as jnp
-import numpy as np
 from jax import lax
 from jax.experimental import pallas as pl
 from jax.experimental.pallas import tpu as pltpu
@@ -21,23 +20,13 @@
 BF16 = jnp.bfloat16
 
 
-def walsh(extent):
-    ids = np.arange(extent)
-    common = ids[:, None] & ids[None, :]
-    parity = np.zeros_like(common)
-    while common.any():
-        parity ^= common & 1
-        common = common >> 1
-    return (1 - 2 * parity).astype(np.float32)
-
-
 def kernel(
     cfg,
-    tok_hbm, gate_hbm, up_hbm, down_hbm, gs_hbm, us_hbm, sb_hbm, ds_ref, walsh_ref,
+    tok_hbm, gate_hbm, up_hbm, down_hbm, gs_hbm, us_hbm, sb_hbm, ds_ref,
     out_ref,
-    tok, wv, dv, fac, part, ring, lr, ar, br, agr, dp, dr,
+    tok, wv, dv, fac, part, ring, lr, ar, br, agr, dp0, dp1, o1x, o1y, v0, v1, o2x, o2y, wtab,
     tok_s, tok_r, tok_o, wa, wb, w_s, wf_s, d_a, d_b, d_s, df_s, fac_r, fac_s,
-    ring_s, ring_r, a_s, a_r, b_s, b_r, g_s, g_r, o_s, o_r,
+    ring_s, ring_r, a_s, a_r, b_s, b_r, g_s, g_r, o_s, o1_r, o2_r,
 ):
     Z, K, NCH = cfg
     NP = K * YL
@@ -77,6 +66,11 @@
         if axis == 0:
             return lax.rem(x + by, NX), y
         return x, lax.rem(y + by, NY)
+
+    bits = lax.broadcasted_iota(jnp.int32, (BLOCK, BLOCK), 0) & lax.broadcasted_iota(jnp.int32, (BLOCK, BLOCK), 1)
+    for by in (4, 2, 1):
+        bits = bits ^ (bits >> by)
+    wtab[...] = (1 - 2 * (bits & 1)).astype(F32).astype(BF16)
 
     barrier = pltpu.get_barrier_semaphore()
     near = [chip(*moved(0, 1)), chip(*moved(0, NX - 1)), chip(*moved(1, 1)), chip(*moved(1, NY - 1)),
@@ -281,7 +275,7 @@
         hidden = gate / (1.0 + jnp.exp(-gate)) * up * (2 * sign - 1).astype(F32)
         hi = hidden.astype(BF16)
         lo = (hidden - hi.astype(F32)).astype(BF16)
-        w = walsh_ref[...]
+        w = wtab[...]
         turned = jnp.dot(hi, w, preferred_element_type=F32) + jnp.dot(lo, w, preferred_element_type=F32)
         turned = (turned * (1.0 / math.sqrt(BLOCK))).astype(BF16)
         for h in range(2):
@@ -348,32 +342,59 @@
             if n + 1 < half:
                 g_copy(d, ch, n + 1).start()
 
-    def o_copy(j, i):
-        p = lax.rem(me + i, NP)
-        return remote(dp.at[j, lax.rem(p, 2), p // 2], dr.at[me, j], o_s.at[i], o_r.at[i], plane(p))
+    here = (x, y)
+    sizes = (NX, NY)
+    quarter = feats // 2
+
+    def o_copy(f, stage, j, i):
+        axis = f if stage == 0 else 1 - f
+        p = lax.rem(here[axis] + i, sizes[axis])
+        dev = chip(p, y) if axis == 0 else chip(x, p)
+        if stage == 0:
+            return remote((dp0, dp1)[f].at[j, p], (o1x, o1y)[f].at[j, here[axis]], o_s.at[f, 0], o1_r.at[f, j], dev)
+        return remote((v0, v1)[f].at[j, p], (o2x, o2y)[f].at[j, here[axis]], o_s.at[f, 1], o2_r.at[f], dev)
 
     def down(j):
-        x = jnp.concatenate(
+        x_all = jnp.concatenate(
             [agr[j, ch, h].reshape(K * ROWS, TILE) for ch in range(NCH) for h in range(2)], axis=1)
         for f in range(2):
-            for q in range(feats // BLOCK):
-                cols = slice(q * BLOCK, (q + 1) * BLOCK)
-                acc = jnp.dot(x, dv[f, :, :, :, cols].reshape(NCH * BLOCK, BLOCK), preferred_element_type=F32)
-                dp[j, f, :, :, cols] = acc.astype(BF16).reshape(K, ROWS, BLOCK)
-
-        def o_start(i, _):
-            o_copy(j, i).start()
+            for e in range(2):
+                cols = slice(f * quarter, (f + 1) * quarter)
+                acc = jnp.dot(x_all, dv[e, :, :, :, cols].reshape(NCH * BLOCK, quarter), preferred_element_type=F32)
+                acc = acc.astype(BF16).reshape(NX, YH, ROWS, quarter)
+                for yh in range(YH):
+                    if f == 0:
+                        dp0[j, :, yh * YL + e] = acc[:, yh]
+                    else:
+                        dp1[j, yh * YL + e] = acc[:, yh]
+            for i in range(1, sizes[f]):
+                o_copy(f, 0, j, i).start()
+        o1x[j, x] = dp0[j, x]
+        o1y[j, y] = dp1[j, y]
+
+    def second(j):
+        for f in range(2):
+            src = (o1x, o1y)[f]
+            got = src.at[j, 1:sizes[f]]
+            pltpu.make_async_copy(got, got, o1_r.at[f, j]).wait()
+            acc = src[j, 0].astype(F32)
+            for q in range(1, sizes[f]):
+                acc += src[j, q].astype(F32)
+            dst = (v0, v1)[f]
+            dst[j] = acc.astype(BF16)
+            for i in range(1, sizes[1 - f]):
+                o_copy(f, 1, j, i).start()
+        o2x[j, y] = v0[j, y]
+        o2y[j, x] = v1[j, x]
+
+    def near(do, n):
+        def one(i, _):
+            do(lax.rem(z + jnp.where(i == 0, Z - 1 - n, 1 + n), Z))
             return 0
 
-        lax.fori_loop(1, NP, o_start, 0)
-        dr[me, j] = dp[j, a, k]
-
-    def down_near(n):
-        def one(i, _):
-            down(lax.rem(z + jnp.where(i == 0, Z - 1 - n, 1 + n), Z))
-            return 0
-
         lax.fori_loop(0, 2 if n < half - 1 else 1, one, 0)
+
+    final = NCH - 1 + half + 2
 
     def slot(t, _):
         def at(n, do):
@@ -394,9 +415,16 @@
         at(0, ring_first)
         for n in range(half - 1, 0, -1):
             at(n, functools.partial(middle, n=n))
-        for n in range(half - 1, -1, -1):
-            at(half + 3 + n, functools.partial(g_take, n=n))
-        at(half + 2, back)
+        for n in range(half, -1, -1):
+            m = final + n - t
+            for ch in (NCH - 1 - 2 * m, NCH - 2 * m):
+                @pl.when(jnp.logical_and(ch >= 0, ch < NCH))
+                def _():
+                    if n > 0:
+                        g_take(ch, n - 1)
+                    else:
+                        back(ch)
+
         at(half + 1, mix)
         at(half, last)
         at(half, a_send)
@@ -411,43 +439,46 @@
             def _():
                 d_forward().start()
 
-        @pl.when(t == NCH - 1 + half + 2)
+        @pl.when(t == final)
         def _():
             down(z)
 
         for n in range(half):
-            @pl.when(t == NCH - 1 + half + 3 + n)
+            @pl.when(t == final + 1 + n)
             def _():
-                down_near(n)
+                if n == 0:
+                    second(z)
+                else:
+                    near(second, n - 1)
+                near(down, n)
 
         return 0
 
     product(0)
-    lax.fori_loop(0, NCH + 2 * half + 2, slot, 0)
-
-    def o_wait(i, _):
-        src = lax.rem(me + NP - i, NP)
-        pltpu.make_async_copy(dr.at[src], dr.at[src], o_r.at[i]).wait()
+    lax.fori_loop(0, final + half + 1, slot, 0)
+    near(second, half - 1)
+
+    for f in range(2):
+        got = (o2x, o2y)[f].at[:, 1:sizes[1 - f]]
+        pltpu.make_async_copy(got, got, o2_r.at[f]).wait()
+
+    def total(j, _):
+        for f in range(2):
+            src = (o2x, o2y)[f]
+            acc = src[j, 0].astype(F32)
+            for q in range(1, sizes[1 - f]):
+                acc += src[j, q].astype(F32)
+            per = quarter // TILE
+            scale = jnp.concatenate([ds_ref[f * per + i:f * per + i + 1, :] for i in range(per)], axis=1)
+            out_ref[pl.ds(pl.multiple_of(j * ROWS, ROWS), ROWS), f * quarter:(f + 1) * quarter] = (
+                acc * (scale.astype(F32) * CODE_SCALE)).astype(BF16)
         return 0
 
-    lax.fori_loop(1, NP, o_wait, 0)
-
-    down_f = jnp.concatenate([ds_ref[i:i + 1, :] for i in range(ds_ref.shape[0])], axis=1).astype(F32) * CODE_SCALE
-
-    def total(j, _):
-        acc = dr[0, j].astype(F32)
-        for q in range(1, NP):
-            acc += dr[q, j].astype(F32)
-        out_ref[pl.ds(pl.multiple_of(j * ROWS, ROWS), ROWS), :] = (acc * down_f).astype(BF16)
-        return 0
-
     lax.fori_loop(0, Z, total, 0)
 
-    def sent(i, _):
-        pltpu.make_async_copy(dr.at[0], dr.at[0], o_s.at[i]).wait()
-        return 0
-
-    lax.fori_loop(1, NP, sent, 0)
+    for f in range(2):
+        for i, out in enumerate(((o1x, o1y)[f].at[:, 1:sizes[f]], (o2x, o2y)[f].at[:, 1:sizes[1 - f]])):
+            pltpu.make_async_copy(out, out, o_s.at[f, i]).wait()
     tok_sent()
 
     def w_sent(ch, _):
@@ -481,13 +512,15 @@
     NCH = width // BLOCK
     NP = K * YL
     half = Z // 2
+    NY = YH * YL
+    NX = NP // NY
     dma = pltpu.SemaphoreType.DMA
     any_spec = pl.BlockSpec(memory_space=pl.ANY)
     vmem_spec = pl.BlockSpec(memory_space=pltpu.VMEM)
     return pl.pallas_call(
         functools.partial(kernel, (Z, K, NCH)),
         out_shape=jax.ShapeDtypeStruct(tokens.shape, BF16),
-        in_specs=[any_spec] * 7 + [vmem_spec] * 2,
+        in_specs=[any_spec] * 7 + [vmem_spec],
         out_specs=vmem_spec,
         scratch_shapes=[
             pltpu.VMEM((2, Z, K, ROWS, feats), BF16),
@@ -500,8 +533,15 @@
             pltpu.VMEM((NCH, NP, ROWS, TILE), BF16),
             pltpu.VMEM((NCH, NP, ROWS, TILE), BF16),
             pltpu.VMEM((Z, NCH, 2, K, ROWS, TILE), BF16),
-            pltpu.VMEM((Z, 2, K, ROWS, feats), BF16),
-            pltpu.VMEM((NP, Z, ROWS, feats), BF16),
+            pltpu.VMEM((Z, NX, NY, ROWS, feats // 2), BF16),
+            pltpu.VMEM((Z, NY, NX, ROWS, feats // 2), BF16),
+            pltpu.VMEM((Z, NX, NY, ROWS, feats // 2), BF16),
+            pltpu.VMEM((Z, NY, NX, ROWS, feats // 2), BF16),
+            pltpu.VMEM((Z, NY, ROWS, feats // 2), BF16),
+            pltpu.VMEM((Z, NX, ROWS, feats // 2), BF16),
+            pltpu.VMEM((Z, NY, ROWS, feats // 2), BF16),
+            pltpu.VMEM((Z, NX, ROWS, feats // 2), BF16),
+            pltpu.VMEM((BLOCK, BLOCK), BF16),
             dma((2, 5, 2, 2)), dma((2, 5, 2, 2)), dma,
             dma((NCH,)), dma((NCH,)), dma((NCH,)), dma((NCH,)),
             dma, dma, dma, dma,
@@ -509,7 +549,7 @@
             dma((2, NCH, half)), dma((2, NCH, half)),
             dma((NCH,)), dma((NCH,)), dma((NCH,)), dma((NCH,)),
             dma((2, NCH, half)), dma((2, NCH, half)),
-            dma((NP,)), dma((NP,)),
+            dma((2, 2)), dma((2, Z)), dma((2,)),
         ],
         compiler_params=pltpu.CompilerParams(
             collective_id=0, has_side_effects=True, vmem_limit_bytes=56 * 1024 * 1024),
@@ -522,7 +562,6 @@
         up_scale.reshape(2 * NCH, TILE),
         sign_bits.reshape(2 * NCH, TILE),
         down_scale.reshape(feats // TILE, TILE),
-        jnp.asarray(walsh(BLOCK), BF16),
     )
 
 

time: 169 us -> 173 us (1.024); the launches traced: 167 us -> 173 us
  Pallas kernels: 165 us -> 172 us
    pallas_call x1, Pallas kernels: 165 us -> 172 us  [on_device(): pl.pallas_call(functools.partial(kernel, (Z, K, NCH)), out_shape=jax.Shap...]
where the time goes in v4:
time: 173 us
  Pallas kernels  172 us (99%)
    pallas_call x1, Pallas kernels, on_device(): pl.pallas_call(functools.partial(kernel, (Z, K, NCH)), out_shape=jax.Shap...  172 us

profile of v4, /device:TPU:2, one launch (start us, length us, event | category | flops | bytes accessed | tf_op | source)
XLA Modules:
  0.0 173.3 jit_solution(6494760019059613264)
XLA Ops:
  0.0 171.7 %shard_map.82 = bf16[128,512]{1,0:T(8,128)(2,1)} custom-call(bf16[8,16,512]{2,1,0:T(8,128)(2,1)} %bitcast.7, bf16[512,1792]{1,0:T(8,128)(2,1)} %gate_hbm.1, bf16[512,1792]{1,0:T(8,128)(2,1)} %up_hbm.1, bf16[7,2,128,512]{3,2,1,0:T(8,128)(2,1)} %bitcast.6, s32[14,128]{1,0:T(8,128)} %bitcast.8, s32[14,128]{1,0:T(8,128)} %bitcast.9, s32[14,128]{1,0:T(8,128)} %bitcast.10, ...), custom_call_target="tpu_custom_call" | custom-call | tf_op jit(solution)/shard_map/pallas_call | solution.py:520
  171.7 1.6 copy.10

commit v5 on v4

--- a/solution.py
+++ b/solution.py
@@ -67,103 +67,74 @@
             return lax.rem(x + by, NX), y
         return x, lax.rem(y + by, NY)
 
+    far = sorted(range(Z), key=lambda step: abs(step - half))
+    place = {step: r for r, step in enumerate(far)}
+    feats = down_hbm.shape[-1]
+    wide = feats // 2
+
+    def tok_own(f, r):
+        return pltpu.make_async_copy(
+            tok_hbm.at[lax.rem(z + far[r], Z), :, f * wide:(f + 1) * wide], tok.at[a, f, x, y // YL, r], tok_o.at[f, r])
+
+    for f in range(2):
+        for r in range(Z):
+            tok_own(f, r).start()
+
     bits = lax.broadcasted_iota(jnp.int32, (BLOCK, BLOCK), 0) & lax.broadcasted_iota(jnp.int32, (BLOCK, BLOCK), 1)
     for by in (4, 2, 1):
         bits = bits ^ (bits >> by)
     wtab[...] = (1 - 2 * (bits & 1)).astype(F32).astype(BF16)
 
     barrier = pltpu.get_barrier_semaphore()
-    near = [chip(*moved(0, 1)), chip(*moved(0, NX - 1)), chip(*moved(1, 1)), chip(*moved(1, NY - 1)),
-            other_core, ring_dev(0), ring_dev(1)]
-    for dev in near:
+    peers = [chip(*moved(0, i)) for i in range(1, NX)] + [chip(*moved(1, i)) for i in range(1, NY)]
+    peers += [other_core, ring_dev(0), ring_dev(1)]
+    for dev in peers:
         pl.semaphore_signal(barrier, inc=1, device_id=dev, device_id_type=MESH)
-    pl.semaphore_wait(barrier, len(near))
-
-    feats = tok.shape[-1]
-    wide = feats // 2
-    tok_own = pltpu.make_async_copy(tok_hbm, tok.at[a, :, k], tok_o)
-
-    def spot(f, cx, cy, rows=slice(None)):
-        return tok.at[lax.rem(cy, YL), rows, cx * YH + cy // YL, :, f * wide:(f + 1) * wide]
-
-    def tok_copy(f, stage, i, d, hop):
+    for f in range(2):
+        for r in range(Z):
+            tok_own(f, r).wait()
+    pl.semaphore_wait(barrier, len(peers))
+
+    here = (x, y)
+    sizes = (NX, NY)
+    some = Z // 2
+
+    def tok_copy(piece, f, stage, i, source=False):
+        rows = pl.ds(piece * some, some)
         axis = f if stage == 0 else 1 - f
-        size = NX if axis == 0 else NY
-        by = 1 if d == 0 else size - 1
-        dev = chip(*moved(axis, by))
-        back = size - 1 if d == 0 else 1
-        cx, cy = moved(axis, back) if hop else (x, y)
-        if stage == 1:
-            if f == 0:
-                cx = lax.rem(x + i, NX)
-            else:
-                cy = lax.rem(y + i, NY)
-        rows = slice(None) if not hop else (slice(0, Z // 2) if d == 0 else slice(Z // 2, Z))
-        sem = (f, 1 + i if stage == 1 else 0, d, hop)
-        dst = spot(f, cx, cy, rows)
-        src = tok_hbm.at[:, :, f * wide:(f + 1) * wide] if stage == 0 and not hop else dst
-        if stage == 1 and not hop and i == 0:
-            src = tok_hbm.at[:, :, f * wide:(f + 1) * wide]
-        return remote(src, dst, tok_s.at[sem], tok_r.at[sem], dev)
-
-    def tok_arrived(f, stage, i, d, hop):
-        axis = f if stage == 0 else 1 - f
-        size = NX if axis == 0 else NY
-        n = 2 if hop else 1
-        by = size - n if d == 0 else n
+        by = sizes[axis] - i if source else i
         cx, cy = moved(axis, by)
-        if stage == 1:
-            if f == 0:
-                cx = lax.rem(x + i, NX)
-            else:
-                cy = lax.rem(y + i, NY)
-        rows = slice(None) if not hop else (slice(0, Z // 2) if d == 0 else slice(Z // 2, Z))
-        sem = (f, 1 + i if stage == 1 else 0, d, hop)
-        ref = spot(f, cx, cy, rows)
-        pltpu.make_async_copy(ref, ref, tok_r.at[sem]).wait()
-
-    def tok_begin():
-        for f in range(2):
-            for d in range(2):
-                tok_copy(f, 0, 0, d, 0).start()
-        tok_own.start()
-        for f in range(2):
-            for d in range(2):
-                tok_copy(f, 1, 0, d, 0).start()
-
-    def tok_relay():
-        for d in range(2):
+        dev = chip(cx, cy)
+        if not source:
+            cx, cy = x, y
+        if stage == 0:
+            ref = tok.at[lax.rem(cy, YL), f, cx, cy // YL, rows]
+        elif f == 0:
+            ref = tok.at[lax.rem(cy, YL), f, :, cy // YL, rows]
+        else:
+            ref = tok.at[:, f, cx, :, rows]
+        sem = (piece, f, stage, i)
+        return remote(ref, ref, tok_s.at[sem], tok_r.at[sem], dev)
+
+    def tok_each(do, piece, stage):
+        for i in (1, 3, 2):
             for f in range(2):
-                tok_arrived(f, 0, 0, d, 0)
-                tok_copy(f, 0, 0, d, 1).start()
-                i = 3 if d == 0 else 1
-                for e in range(2):
-                    tok_copy(f, 1, i, e, 0).start()
-        for f in range(2):
-            for d in range(2):
-                tok_arrived(f, 0, 0, d, 1)
-            for e in range(2):
-                tok_copy(f, 1, 2, e, 0).start()
-        for i in (0, 3, 1, 2):
-            for f in range(2):
-                for d in range(2):
-                    tok_arrived(f, 1, i, d, 0)
-                    tok_copy(f, 1, i, d, 1).start()
-        for i in (0, 3, 1, 2):
-            for f in range(2):
-                for d in range(2):
-                    tok_arrived(f, 1, i, d, 1)
-        tok_own.wait()
+                if i < sizes[f if stage == 0 else 1 - f]:
+                    do(piece, f, stage, i)
+
+    def tok_send(piece, stage):
+        tok_each(lambda *at: tok_copy(*at).start(), piece, stage)
+
+    def tok_take(piece, stage):
+        tok_each(lambda *at: tok_copy(*at, source=True).wait_recv(), piece, stage)
 
     def tok_sent():
-        for f in range(2):
-            for d in range(2):
-                for hop in range(2):
-                    tok_copy(f, 0, 0, d, hop).wait_send()
-                    for i in range(4):
-                        tok_copy(f, 1, i, d, hop).wait_send()
-
-    tok_begin()
+        for piece in range(2):
+            for stage in range(2):
+                tok_each(lambda *at: tok_copy(*at).wait_send(), piece, stage)
+
+    tok_send(0, 0)
+    tok_send(1, 0)
 
     def chunk_of(ref, ch):
         return ref.at[:, pl.ds(pl.multiple_of(ch * BLOCK, BLOCK), BLOCK)]
@@ -211,37 +182,43 @@
             pltpu.make_async_copy(ref, fac.at[i], fac_r.at[i]).start()
             remote(ref, fac.at[i], fac_s.at[i], fac_r.at[i], other_core).start()
 
-    tok_relay()
+    for piece in range(2):
+        tok_take(piece, 0)
+        tok_send(piece, 1)
+    tok_take(0, 1)
     for ch in range(1, ahead):
         w_start(ch)
     for i in range(3):
         pltpu.make_async_copy(fac.at[i], fac.at[i], fac_r.at[i]).wait()
 
     def ring_copy(d, ch, n):
-        step = half - n if d == 0 else Z - half + n
-        j = lax.rem(z + step, Z)
+        j = place[half - n if d == 0 else Z - half + n]
         if n == 0:
             return remote(part.at[ch, j, d], ring.at[d, ch, n, d], ring_s.at[d, ch, n], ring_r.at[d, ch, n], ring_dev(d))
         return remote(part.at[ch, j], ring.at[d, ch, n], ring_s.at[d, ch, n], ring_r.at[d, ch, n], ring_dev(d))
 
-    def product(ch):
-        w_wait(ch)
-
-        @pl.when(diag)
-        def _():
-            w_forward(ch).start()
-
+    def product_rows(ch, lo, hi):
         def rows(m, _):
             for g in range(2):
                 acc = jnp.zeros((2 * K * ROWS, BLOCK), F32)
                 for f in range(2):
-                    x = tok[f, pl.ds(2 * m, 2)].reshape(2 * K * ROWS, -1)
-                    acc += jnp.dot(x, wv[ch, f, g], preferred_element_type=F32)
+                    for q in range(2):
+                        xs = [tok[f, q, :, :, 2 * m + e].reshape(K * ROWS, wide) for e in range(2)]
+                        acc += jnp.dot(jnp.concatenate(xs, axis=0), wv[ch, f, g, q * wide:(q + 1) * wide],
+                                       preferred_element_type=F32)
                 part[ch, pl.ds(2 * m, 2), g] = acc.astype(BF16).reshape(2, K * ROWS, BLOCK)
             return 0
 
-        lax.fori_loop(0, Z // 2, rows, 0)
-
+        lax.fori_loop(lo // 2, hi // 2, rows, 0)
+
+    def w_take(ch):
+        w_wait(ch)
+
+        @pl.when(diag)
+        def _():
+            w_forward(ch).start()
+
+    def w_next(ch):
         @pl.when(ch + ahead < NCH)
         def _():
             w_start(ch + ahead)
@@ -249,12 +226,20 @@
         @pl.when(ch == NCH - 1)
         def _():
             d_start()
+
+    def product(ch):
+        w_take(ch)
+        product_rows(ch, 0, Z)
+        w_next(ch)
+
+    def ring_first(ch):
+        for d in range(2):
+            ring_copy(d, ch, 0).start()
 
     def middle(ch, n):
         for d in range(2):
             ring_copy(d, ch, n - 1).wait_recv()
-            step = half - n if d == 0 else Z - half + n
-            j = lax.rem(z + step, Z)
+            j = place[half - n if d == 0 else Z - half + n]
             for g in ((d,) if n == 1 else (0, 1)):
                 part[ch, j, g] = (part[ch, j, g].astype(F32) + ring[d, ch, n - 1, g].astype(F32)).astype(BF16)
             ring_copy(d, ch, n).start()
@@ -264,7 +249,7 @@
         for d in range(2):
             ring_copy(d, ch, n).wait_recv()
         sums = [
-            part[ch, z, g].astype(F32) + ring[0, ch, n, g].astype(F32) + ring[1, ch, n, g].astype(F32)
+            part[ch, place[0], g].astype(F32) + ring[0, ch, n, g].astype(F32) + ring[1, ch, n, g].astype(F32)
             for g in range(2)
         ]
         gate_f, up_f, sign = [
@@ -342,9 +327,7 @@
             if n + 1 < half:
                 g_copy(d, ch, n + 1).start()
 
-    here = (x, y)
-    sizes = (NX, NY)
-    quarter = feats // 2
+    quarter = wide
 
     def o_copy(f, stage, j, i):
         axis = f if stage == 0 else 1 - f
@@ -404,10 +387,6 @@
             def _():
                 do(ch)
 
-        def ring_first(ch):
-            for d in range(2):
-                ring_copy(d, ch, 0).start()
-
         def back(ch):
             all_others(b_r.at[ch])
             g_send(ch, 0)
@@ -416,15 +395,7 @@
         for n in range(half - 1, 0, -1):
             at(n, functools.partial(middle, n=n))
         for n in range(half, -1, -1):
-            m = final + n - t
-            for ch in (NCH - 1 - 2 * m, NCH - 2 * m):
-                @pl.when(jnp.logical_and(ch >= 0, ch < NCH))
-                def _():
-                    if n > 0:
-                        g_take(ch, n - 1)
-                    else:
-                        back(ch)
-
+            at(half + 2 + n, functools.partial(g_take, n=n - 1) if n else back)
         at(half + 1, mix)
         at(half, last)
         at(half, a_send)
@@ -446,16 +417,22 @@
         for n in range(half):
             @pl.when(t == final + 1 + n)
             def _():
+                near(down, n)
                 if n == 0:
                     second(z)
                 else:
                     near(second, n - 1)
-                near(down, n)
 
         return 0
 
-    product(0)
-    lax.fori_loop(0, final + half + 1, slot, 0)
+    w_take(0)
+    product_rows(0, 0, some)
+    ring_first(0)
+    tok_take(1, 1)
+    product_rows(0, some, Z)
+    w_next(0)
+    product(1)
+    lax.fori_loop(1, final + half + 1, slot, 0)
     near(second, half - 1)
 
     for f in range(2):
@@ -523,7 +500,7 @@
         in_specs=[any_spec] * 7 + [vmem_spec],
         out_specs=vmem_spec,
         scratch_shapes=[
-            pltpu.VMEM((2, Z, K, ROWS, feats), BF16),
+            pltpu.VMEM((2, 2, NX, YH, Z, ROWS, feats // 2), BF16),
             pltpu.VMEM((NCH, 2, 2, feats, BLOCK), BF16),
             pltpu.VMEM((2, NCH, 2, TILE, feats), BF16),
             pltpu.VMEM((3, 2 * NCH, TILE), jnp.int32),
@@ -542,7 +519,7 @@
             pltpu.VMEM((Z, NY, ROWS, feats // 2), BF16),
             pltpu.VMEM((Z, NX, ROWS, feats // 2), BF16),
             pltpu.VMEM((BLOCK, BLOCK), BF16),
-            dma((2, 5, 2, 2)), dma((2, 5, 2, 2)), dma,
+            dma((2, 2, 2, 4)), dma((2, 2, 2, 4)), dma((2, Z)),
             dma((NCH,)), dma((NCH,)), dma((NCH,)), dma((NCH,)),
             dma, dma, dma, dma,
             dma((3,)), dma((3,)),

time: 173 us -> 165 us (0.954)
  Pallas kernels: 172 us -> 163 us
    pallas_call x1, Pallas kernels: 172 us -> 163 us  [on_device(): pl.pallas_call(functools.partial(kernel, (Z, K, NCH)), out_shape=jax.Shap...]
where the time goes in v5:
time: 165 us
  Pallas kernels  163 us (99%)
    pallas_call x1, Pallas kernels, on_device(): pl.pallas_call(functools.partial(kernel, (Z, K, NCH)), out_shape=jax.Shap...  163 us

profile of v5, /device:TPU:2, one launch (start us, length us, event | category | flops | bytes accessed | tf_op | source)
XLA Modules:
  0.0 164.7 jit_solution(14255258269218388763)
XLA Ops:
  0.0 163.1 %shard_map.82 = bf16[128,512]{1,0:T(8,128)(2,1)} custom-call(bf16[8,16,512]{2,1,0:T(8,128)(2,1)} %bitcast.7, bf16[512,1792]{1,0:T(8,128)(2,1)} %gate_hbm.1, bf16[512,1792]{1,0:T(8,128)(2,1)} %up_hbm.1, bf16[7,2,128,512]{3,2,1,0:T(8,128)(2,1)} %bitcast.6, s32[14,128]{1,0:T(8,128)} %bitcast.8, s32[14,128]{1,0:T(8,128)} %bitcast.9, s32[14,128]{1,0:T(8,128)} %bitcast.10, ...), custom_call_target="tpu_custom_call" | custom-call | tf_op jit(solution)/shard_map/pallas_call | solution.py:497
  163.1 1.6 copy.10

commit v6 on v5

--- a/solution.py
+++ b/solution.py
@@ -67,29 +67,30 @@
             return lax.rem(x + by, NX), y
         return x, lax.rem(y + by, NY)
 
-    far = sorted(range(Z), key=lambda step: abs(step - half))
-    place = {step: r for r, step in enumerate(far)}
-    feats = down_hbm.shape[-1]
-    wide = feats // 2
-
-    def tok_own(f, r):
-        return pltpu.make_async_copy(
-            tok_hbm.at[lax.rem(z + far[r], Z), :, f * wide:(f + 1) * wide], tok.at[a, f, x, y // YL, r], tok_o.at[f, r])
-
-    for f in range(2):
-        for r in range(Z):
-            tok_own(f, r).start()
-
-    bits = lax.broadcasted_iota(jnp.int32, (BLOCK, BLOCK), 0) & lax.broadcasted_iota(jnp.int32, (BLOCK, BLOCK), 1)
-    for by in (4, 2, 1):
-        bits = bits ^ (bits >> by)
-    wtab[...] = (1 - 2 * (bits & 1)).astype(F32).astype(BF16)
-
     barrier = pltpu.get_barrier_semaphore()
     peers = [chip(*moved(0, i)) for i in range(1, NX)] + [chip(*moved(1, i)) for i in range(1, NY)]
     peers += [other_core, ring_dev(0), ring_dev(1)]
     for dev in peers:
         pl.semaphore_signal(barrier, inc=1, device_id=dev, device_id_type=MESH)
+
+    far = sorted(range(Z), key=lambda step: abs(step - half))
+    place = {step: r for r, step in enumerate(far)}
+    feats = down_hbm.shape[-1]
+    wide = feats // 2
+
+    def tok_own(f, r):
+        return pltpu.make_async_copy(
+            tok_hbm.at[lax.rem(z + far[r], Z), :, f * wide:(f + 1) * wide], tok.at[a, f, x, y // YL, r], tok_o.at[f, r])
+
+    for f in range(2):
+        for r in range(Z):
+            tok_own(f, r).start()
+
+    bits = lax.broadcasted_iota(jnp.int32, (BLOCK, BLOCK), 0) & lax.broadcasted_iota(jnp.int32, (BLOCK, BLOCK), 1)
+    for by in (4, 2, 1):
+        bits = bits ^ (bits >> by)
+    wtab[...] = (1 - 2 * (bits & 1)).astype(F32).astype(BF16)
+
     for f in range(2):
         for r in range(Z):
             tok_own(f, r).wait()
@@ -170,6 +171,10 @@
         def _():
             remote(down_hbm, dv.at[a], d_s, d_b, other_y).start()
 
+    def d_wait():
+        pltpu.make_async_copy(dv.at[a], dv.at[a], d_a).wait()
+        pltpu.make_async_copy(dv.at[1 - a], dv.at[1 - a], d_b).wait()
+
     def d_forward():
         return remote(dv.at[1 - a], dv.at[1 - a], df_s, d_b, other_core)
 
@@ -185,9 +190,9 @@
     for piece in range(2):
         tok_take(piece, 0)
         tok_send(piece, 1)
-    tok_take(0, 1)
     for ch in range(1, ahead):
         w_start(ch)
+    tok_take(0, 1)
     for i in range(3):
         pltpu.make_async_copy(fac.at[i], fac.at[i], fac_r.at[i]).wait()
 
@@ -401,14 +406,16 @@
         at(half, a_send)
         at(-1, product)
 
-        @pl.when(t == NCH + half - 1)
-        def _():
-            pltpu.make_async_copy(dv.at[a], dv.at[a], d_a).wait()
-            pltpu.make_async_copy(dv.at[1 - a], dv.at[1 - a], d_b).wait()
-
+        @pl.when(t == final - 2)
+        def _():
             @pl.when(diag)
             def _():
+                d_wait()
                 d_forward().start()
+
+        @pl.when(jnp.logical_and(t == final, jnp.logical_not(diag)))
+        def _():
+            d_wait()
 
         @pl.when(t == final)
         def _():

time: 165 us -> 164 us (level)
  no operation moved by 1% of the time
where the time goes in v6:
time: 164 us
  Pallas kernels  162 us (99%)
    pallas_call x1, Pallas kernels, on_device(): pl.pallas_call(functools.partial(kernel, (Z, K, NCH)), out_shape=jax.Shap...  162 us

profile of v6, /device:TPU:2, one launch (start us, length us, event | category | flops | bytes accessed | tf_op | source)
XLA Modules:
  0.0 163.8 jit_solution(8244942537336183925)
XLA Ops:
  0.0 162.2 %shard_map.82 = bf16[128,512]{1,0:T(8,128)(2,1)} custom-call(bf16[8,16,512]{2,1,0:T(8,128)(2,1)} %bitcast.7, bf16[512,1792]{1,0:T(8,128)(2,1)} %gate_hbm.1, bf16[512,1792]{1,0:T(8,128)(2,1)} %up_hbm.1, bf16[7,2,128,512]{3,2,1,0:T(8,128)(2,1)} %bitcast.6, s32[14,128]{1,0:T(8,128)} %bitcast.8, s32[14,128]{1,0:T(8,128)} %bitcast.9, s32[14,128]{1,0:T(8,128)} %bitcast.10, ...), custom_call_target="tpu_custom_call" | custom-call | tf_op jit(solution)/shard_map/pallas_call | solution.py:504
  162.2 1.6 copy.10
